TPU v7x, 32 devices: a whole 2x2x4 slice. The times are simulated.
32 devices in a mesh: shard: 4 (over y, x), dp: 4 (over z), tensor: 2 (over core).
Axes of the slice: x: 2, y: 2, z: 4, core: 2. Of those that a mesh axis runs over, the one named last changes fastest.
Arguments:
- tokens: bfloat16 [9456, 768], P(('shard', 'dp')), may hold values from -6 to 6
- routes: int32 [2, 9456, 2], P(None, ('shard', 'dp')), may hold values from 0 to 7, all different within a row; in each aligned block of 591 rows (0 to 590, 591 to 1181, ..., all dimensions but the last counted through in order) at most 185 rows name the same one
- w_qkv: bfloat16 [2, 768, 3, 768], P(None, ('shard', 'dp'), None, 'tensor'), may hold values from -0.21875 to 0.21875
- w_out: bfloat16 [2, 768, 768], P(None, ('shard', 'dp'), 'tensor'), may hold values from -1.25 to 1.25
- w_router: bfloat16 [2, 768, 8], P(None, ('shard', 'dp')), may hold values from -0.15625 to 0.15625
- ln_gain: bfloat16 [2, 768, 2], P(None, ('shard', 'dp')), may hold values from 0.5 to 1.5
- ln_shift: bfloat16 [2, 768, 2], P(None, ('shard', 'dp')), may hold values from -0.8984375 to 0.8984375
- expert_in: bfloat16 [2, 8, 768, 3072], P(None, 'shard', 'dp', 'tensor'), may hold values from -0.21875 to 0.21875
- expert_out: bfloat16 [2, 8, 768, 3072], P(None, 'shard', 'dp', 'tensor'), may hold values from -0.109375 to 0.109375
- cotangent: bfloat16 [9456, 768], P(('shard', 'dp')), may hold values from -6 to 6
Outputs:
- mixed: bfloat16 [9456, 768], P(('shard', 'dp'))
- tokens_grad: float32 [9456, 768], P(('shard', 'dp'))
- w_qkv_grad: float32 [2, 768, 3, 768], P(None, ('shard', 'dp'), None, 'tensor')
- w_out_grad: float32 [2, 768, 768], P(None, ('shard', 'dp'), 'tensor')
- w_router_grad: float32 [2, 768, 8], P(None, ('shard', 'dp'))
- ln_gain_grad: float32 [2, 768, 2], P(None, ('shard', 'dp'))
- ln_shift_grad: float32 [2, 768], P(None, ('shard', 'dp'))
- second_shift_grad: float32 [2, 768], P(None, ('shard', 'dp'))
- expert_in_grad: float32 [2, 8, 768, 3072], P(None, 'shard', 'dp', 'tensor')
- expert_out_grad: float32 [2, 8, 768, 3072], P(None, 'shard', 'dp', 'tensor')
Inputs may be any that keep to these rules, and one draw needn't show every extreme that they name: `routes`: in the rows of one index of shard and dp and one block, no expert is named more than 185 times; a token's two experts differ.
All inputs are finite; a program needn't handle non-finite values.
Results may differ from a plain program's by a relative error of at most 0.02.
Values may be sent and summed in bfloat16 or wider, within the bound.
A program may use at most 256 MiB of HBM per device.

v0:
```python
import jax
import jax.numpy as jnp
from jax import lax
from jax.sharding import PartitionSpec as P

D = 768
HEAD_DIM = 64
SEQ = 197
LAYERS = 2


def norm_rows(values, gain_vec, shift_vec):
    row_mean = jnp.mean(values, axis=-1, keepdims=True)
    centred = values - row_mean
    variance = jnp.mean(centred * centred, axis=-1, keepdims=True)
    return centred * lax.rsqrt(variance + 1e-06) * gain_vec + shift_vec


def gelu_exact(values):
    return jax.nn.gelu(values, approximate=False)


def route_slots(route_rows, experts, capacity):
    flat_ids = route_rows.reshape(-1)
    onehot_hits = (flat_ids[:, None] == jnp.arange(experts, dtype=jnp.int32)[None, :]).astype(
        jnp.int32
    )
    earlier = jnp.cumsum(onehot_hits, axis=0, dtype=jnp.int32) - onehot_hits
    return flat_ids * capacity + jnp.sum(earlier * onehot_hits, axis=1)


def on_device(
    tokens, routes, w_qkv, w_out, w_router, ln_gain, ln_shift, expert_in, expert_out, cotangent
):
    tok_dev = tokens.shape[0]
    images = tok_dev // SEQ
    shards = lax.axis_size("shard")
    exp_dev = expert_in.shape[1]
    experts = exp_dev * shards
    capacity = 5 * tok_dev // (2 * experts) + 1
    local_width = w_qkv.shape[3]
    heads_dev = local_width // HEAD_DIM
    score_scale = HEAD_DIM ** (-0.5)
    expert_ids = jnp.arange(experts, dtype=jnp.int32)
    stream = tokens.astype(jnp.float32)
    stored = []
    for depth in range(LAYERS):
        proj_qkv, proj_out, router, gain_pair, shift_pair = (
            lax.all_gather(w_qkv[depth], ("shard", "dp"), axis=0, tiled=True),
            lax.all_gather(w_out[depth], ("shard", "dp"), axis=0, tiled=True),
            lax.all_gather(w_router[depth], ("shard", "dp"), axis=0, tiled=True),
            lax.all_gather(ln_gain[depth], ("shard", "dp"), axis=0, tiled=True),
            lax.all_gather(ln_shift[depth], ("shard", "dp"), axis=0, tiled=True),
        )
        weight_in, weight_down = (
            lax.all_gather(expert_in[depth], "dp", axis=1, tiled=True),
            lax.all_gather(expert_out[depth], "dp", axis=1, tiled=True),
        )
        gain_pair = gain_pair.astype(jnp.float32)
        shift_pair = shift_pair.astype(jnp.float32)
        normed_in = norm_rows(stream, gain_pair[:, 0], shift_pair[:, 0]).astype(jnp.bfloat16)
        packed = jnp.einsum(
            "td,dcf->tcf", normed_in, proj_qkv, preferred_element_type=jnp.float32
        ).astype(jnp.bfloat16)
        packed = packed.reshape(images, SEQ, 3, heads_dev, HEAD_DIM)
        query_rows, key_rows, value_rows = (packed[:, :, 0], packed[:, :, 1], packed[:, :, 2])
        scores = (
            jnp.einsum("bqhd,bkhd->bhqk", query_rows, key_rows, preferred_element_type=jnp.float32)
            * score_scale
        )
        row_max = jnp.max(scores, axis=-1, keepdims=True)
        exponent = jnp.exp(scores - row_max)
        row_total = jnp.sum(exponent, axis=-1, keepdims=True)
        log_total = row_max + jnp.log(row_total)
        probs_low = (exponent / row_total).astype(jnp.bfloat16)
        heads_out = jnp.einsum(
            "bhqk,bkhd->bqhd", probs_low, value_rows, preferred_element_type=jnp.float32
        )
        heads_out = heads_out.reshape(tok_dev, local_width).astype(jnp.bfloat16)
        partial_attn = lax.dot_general(
            heads_out, proj_out, (((1,), (1,)), ((), ())), preferred_element_type=jnp.float32
        )
        attention = lax.psum(partial_attn, "tensor")
        middle = stream + attention
        act_in = norm_rows(middle, gain_pair[:, 1], shift_pair[:, 1]).astype(jnp.bfloat16)
        logits = jnp.dot(act_in, router, preferred_element_type=jnp.float32)
        route_ids = routes[depth]
        onehot_hits = (route_ids[:, :, None] == expert_ids[None, None, :]).astype(jnp.float32)
        chosen = jnp.sum(onehot_hits * logits[:, None, :], axis=-1)
        chosen_max = jnp.max(chosen, axis=-1, keepdims=True)
        chosen_exp = jnp.exp(chosen - chosen_max)
        gate_probs = chosen_exp / jnp.sum(chosen_exp, axis=-1, keepdims=True)
        dest_rows = route_slots(route_ids, experts, capacity)
        outgoing = (
            jnp.zeros((experts * capacity, D), jnp.bfloat16)
            .at[dest_rows]
            .set(jnp.repeat(act_in, 2, axis=0))
        )
        received = lax.all_to_all(
            outgoing.reshape(shards, exp_dev, capacity, D),
            "shard",
            split_axis=0,
            concat_axis=0,
            tiled=True,
        )
        pre_act = jnp.einsum(
            "secd,edf->secf", received, weight_in, preferred_element_type=jnp.float32
        )
        act_low = gelu_exact(pre_act).astype(jnp.bfloat16)
        expert_y = jnp.einsum(
            "secf,edf->secd", act_low, weight_down, preferred_element_type=jnp.float32
        )
        returned = lax.all_to_all(
            expert_y.astype(jnp.bfloat16), "shard", split_axis=0, concat_axis=0, tiled=True
        ).astype(expert_y.dtype)
        token_out = returned.reshape(experts * capacity, D)[dest_rows].reshape(tok_dev, 2, D)
        partial_moe = jnp.sum(gate_probs[:, :, None] * token_out, axis=1)
        mixture_out = lax.psum(partial_moe.astype(jnp.bfloat16), "tensor").astype(jnp.float32)
        stored.append(
            (
                stream,
                middle,
                proj_qkv,
                proj_out,
                router,
                gain_pair,
                shift_pair,
                weight_in,
                weight_down,
                normed_in,
                query_rows,
                key_rows,
                value_rows,
                log_total,
                heads_out,
                act_in,
                onehot_hits,
                gate_probs,
                dest_rows,
                received,
                pre_act,
                token_out,
            )
        )
        stream = middle + mixture_out
    mixed = stream.astype(jnp.bfloat16)
    stream_grad = cotangent.astype(jnp.float32)
    block_results = [None] * LAYERS
    expert_results = [None] * LAYERS
    for depth in reversed(range(LAYERS)):
        (
            stream_in,
            middle,
            proj_qkv,
            proj_out,
            router,
            gain_pair,
            shift_pair,
            weight_in,
            weight_down,
            normed_in,
            query_rows,
            key_rows,
            value_rows,
            log_total,
            heads_out,
            act_in,
            onehot_hits,
            gate_probs,
            dest_rows,
            received,
            pre_act,
            token_out,
        ) = stored[depth]
        weight_in, weight_down = (
            lax.all_gather(expert_in[depth], "dp", axis=1, tiled=True),
            lax.all_gather(expert_out[depth], "dp", axis=1, tiled=True),
        )
        out_grads = (
            (gate_probs[:, :, None] * stream_grad[:, None, :])
            .reshape(2 * tok_dev, D)
            .astype(jnp.bfloat16)
        )
        grad_out = jnp.zeros((experts * capacity, D), jnp.bfloat16).at[dest_rows].set(out_grads)
        grad_in = lax.all_to_all(
            grad_out.reshape(shards, exp_dev, capacity, D),
            "shard",
            split_axis=0,
            concat_axis=0,
            tiled=True,
        )
        act_low = gelu_exact(pre_act).astype(jnp.bfloat16)
        act_grad = jnp.einsum(
            "secd,edf->secf", grad_in, weight_down, preferred_element_type=jnp.float32
        )
        down_grad = jnp.einsum(
            "secd,secf->edf", grad_in, act_low, preferred_element_type=jnp.float32
        )
        gelu_value, gelu_pull = jax.vjp(gelu_exact, pre_act)
        pre_grad = gelu_pull(act_grad)[0].astype(jnp.bfloat16)
        in_grad = jnp.einsum(
            "secd,secf->edf", received, pre_grad, preferred_element_type=jnp.float32
        )
        rows_grad = jnp.einsum(
            "secf,edf->secd", pre_grad, weight_in, preferred_element_type=jnp.float32
        )
        rows_back = lax.all_to_all(
            rows_grad.astype(jnp.bfloat16), "shard", split_axis=0, concat_axis=0, tiled=True
        ).astype(rows_grad.dtype)
        partial_act = jnp.sum(
            rows_back.reshape(experts * capacity, D)[dest_rows].reshape(tok_dev, 2, D), axis=1
        )
        partial_gate = jnp.sum(stream_grad[:, None, :] * token_out, axis=-1)
        act_grad_sum, gate_grad = (
            lax.psum(partial_act.astype(jnp.bfloat16), "tensor").astype(jnp.float32),
            lax.psum(partial_gate.astype(jnp.bfloat16), "tensor").astype(jnp.float32),
        )
        chosen_grad = gate_probs * (
            gate_grad - jnp.sum(gate_probs * gate_grad, axis=-1, keepdims=True)
        )
        logit_grad = jnp.sum(onehot_hits * chosen_grad[:, :, None], axis=1)
        router_grad = jnp.dot(
            act_in.astype(jnp.float32).T, logit_grad, precision=lax.Precision.HIGHEST
        )
        act_grad_sum = act_grad_sum + jnp.dot(
            logit_grad, router.astype(jnp.float32).T, precision=lax.Precision.HIGHEST
        )
        norm_value, norm_pull = jax.vjp(norm_rows, middle, gain_pair[:, 1], shift_pair[:, 1])
        middle_term, second_gain, second_shift = norm_pull(act_grad_sum)
        middle_grad = stream_grad + middle_term
        attn_grad = middle_grad.astype(jnp.bfloat16)
        out_proj_grad = lax.dot_general(
            attn_grad, heads_out, (((0,), (0,)), ((), ())), preferred_element_type=jnp.float32
        )
        heads_grad = jnp.dot(attn_grad, proj_out, preferred_element_type=jnp.float32).astype(
            jnp.bfloat16
        )
        heads_grad = heads_grad.reshape(images, SEQ, heads_dev, HEAD_DIM)
        scores = (
            jnp.einsum("bqhd,bkhd->bhqk", query_rows, key_rows, preferred_element_type=jnp.float32)
            * score_scale
        )
        probs_full = jnp.exp(scores - log_total)
        probs_low = probs_full.astype(jnp.bfloat16)
        value_grad = jnp.einsum(
            "bhqk,bqhd->bkhd", probs_low, heads_grad, preferred_element_type=jnp.float32
        )
        probs_grad = jnp.einsum(
            "bqhd,bkhd->bhqk", heads_grad, value_rows, preferred_element_type=jnp.float32
        )
        score_grad = probs_full * (
            probs_grad - jnp.sum(probs_full * probs_grad, axis=-1, keepdims=True)
        )
        score_grad = score_grad.astype(jnp.bfloat16)
        query_grad = (
            jnp.einsum("bhqk,bkhd->bqhd", score_grad, key_rows, preferred_element_type=jnp.float32)
            * score_scale
        )
        key_grad = (
            jnp.einsum(
                "bhqk,bqhd->bkhd", score_grad, query_rows, preferred_element_type=jnp.float32
            )
            * score_scale
        )
        packed_grad = jnp.stack([query_grad, key_grad, value_grad], axis=2)
        packed_grad = packed_grad.reshape(tok_dev, 3, local_width).astype(jnp.bfloat16)
        qkv_grad = jnp.einsum(
            "td,tcf->dcf", normed_in, packed_grad, preferred_element_type=jnp.float32
        )
        partial_norm = jnp.einsum(
            "tcf,dcf->td", packed_grad, proj_qkv, preferred_element_type=jnp.float32
        )
        normed_grad = lax.psum(partial_norm.astype(jnp.bfloat16), "tensor").astype(jnp.float32)
        first_value, first_pull = jax.vjp(norm_rows, stream_in, gain_pair[:, 0], shift_pair[:, 0])
        stream_term, first_gain, first_shift = first_pull(normed_grad)
        stream_grad = middle_grad + stream_term
        gain_grads = jnp.stack([first_gain, second_gain], axis=1)
        shift_grads = jnp.stack([first_shift, second_shift], axis=1)
        block_results[depth] = (
            lax.psum_scatter(qkv_grad, ("shard", "dp"), scatter_dimension=0, tiled=True),
            lax.psum_scatter(out_proj_grad, ("shard", "dp"), scatter_dimension=0, tiled=True),
            lax.psum_scatter(router_grad, ("shard", "dp"), scatter_dimension=0, tiled=True),
            lax.psum_scatter(gain_grads, ("shard", "dp"), scatter_dimension=0, tiled=True),
            lax.psum_scatter(shift_grads, ("shard", "dp"), scatter_dimension=0, tiled=True),
        )
        expert_results[depth] = (
            lax.psum_scatter(
                in_grad.astype(jnp.bfloat16), "dp", scatter_dimension=1, tiled=True
            ).astype(jnp.float32),
            lax.psum_scatter(
                down_grad.astype(jnp.bfloat16), "dp", scatter_dimension=1, tiled=True
            ).astype(jnp.float32),
        )
    w_qkv_grad = jnp.stack([item[0] for item in block_results], axis=0)
    w_out_grad = jnp.stack([item[1] for item in block_results], axis=0)
    w_router_grad = jnp.stack([item[2] for item in block_results], axis=0)
    ln_gain_grad = jnp.stack([item[3] for item in block_results], axis=0)
    both_shift_grad = jnp.stack([item[4] for item in block_results], axis=0)
    expert_in_grad = jnp.stack([item[0] for item in expert_results], axis=0)
    expert_out_grad = jnp.stack([item[1] for item in expert_results], axis=0)
    ln_shift_grad = both_shift_grad[:, :, 0]
    second_shift_grad = both_shift_grad[:, :, 1]
    return (
        mixed,
        stream_grad,
        w_qkv_grad,
        w_out_grad,
        w_router_grad,
        ln_gain_grad,
        ln_shift_grad,
        second_shift_grad,
        expert_in_grad,
        expert_out_grad,
    )


def solution(mesh):
    placed = (
        P(("shard", "dp"), None),
        P(None, ("shard", "dp"), None),
        P(None, ("shard", "dp"), None, "tensor"),
        P(None, ("shard", "dp"), "tensor"),
        P(None, ("shard", "dp"), None),
        P(None, ("shard", "dp"), None),
        P(None, ("shard", "dp"), None),
        P(None, "shard", "dp", "tensor"),
        P(None, "shard", "dp", "tensor"),
        P(("shard", "dp"), None),
    )
    return jax.shard_map(
        on_device,
        mesh=mesh,
        in_specs=placed,
        out_specs=(
            P(("shard", "dp"), None),
            P(("shard", "dp"), None),
            P(None, ("shard", "dp"), None, "tensor"),
            P(None, ("shard", "dp"), "tensor"),
            P(None, ("shard", "dp"), None),
            P(None, ("shard", "dp"), None),
            P(None, ("shard", "dp")),
            P(None, ("shard", "dp")),
            P(None, "shard", "dp", "tensor"),
            P(None, "shard", "dp", "tensor"),
        ),
        check_vma=False,
    )
```

profile of v0, /device:TPU:0, one launch (start us, length us, event | category | flops | bytes accessed | tf_op | source)
XLA Modules:
  0.0 2841.6 jit_solution(9082871746705810674)
XLA Ops:
  11.2 46.8 %all-gather = bf16[1,768,2]{2,0,1:T(2,128)(2,1)S(1)} all-gather(bf16[1,48,2]{2,0,1:T(2,128)(2,1)S(1)} %copy.520), channel_id=2, replica_groups=mesh['shard'=4,'dp'=4,'tensor'=2] {'shard','dp'}, dimensions={1}, use_global_device_ids=true | all-gather | bytes 3264 | tf_op jit(solution)/shard_map/all_gather | solution.py:52
  59.8 40.6 %all-gather.1 = bf16[1,768,2]{2,0,1:T(2,128)(2,1)S(1)} all-gather(bf16[1,48,2]{2,0,1:T(2,128)(2,1)S(1)} %copy.521), channel_id=3, replica_groups=mesh['shard'=4,'dp'=4,'tensor'=2] {'shard','dp'}, dimensions={1}, use_global_device_ids=true | all-gather | bytes 3264 | tf_op jit(solution)/shard_map/all_gather | solution.py:53
  102.9 43.6 %all-gather.3 = bf16[1,768,384]{2,1,0:T(8,128)(2,1)S(1)} all-gather(bf16[1,48,384]{2,1,0:T(8,128)(2,1)S(1)} %get-tuple-element.63), channel_id=5, replica_groups=mesh['shard'=4,'dp'=4,'tensor'=2] {'shard','dp'}, dimensions={1}, use_global_device_ids=true | all-gather | bytes 626688 | tf_op jit(solution)/shard_map/all_gather | solution.py:50
  179.0 8.9 all-reduce.11.cloned.1.call-done
  196.1 10.3 scatter_custom_fusion
  219.5 25.1 all-to-all-done
  244.6 15.2 all-gather.23.cloned.1.call-done
  259.8 27.9 fusion.19
  287.7 61.9 %all-gather.25.cloned.1.call-done = bf16[1,2,768,1536]{3,2,1,0:T(8,128)(2,1)} async-done(((bf16[1,2,192,1536]{3,2,1,0:T(8,128)(2,1)}), bf16[1,2,768,1536]{3,2,1,0:T(8,128)(2,1)}) %all-gather.25.cloned.1.call-update) | async-done | bytes 4718608 | tf_op jit(solution)/shard_map/all_gather | solution.py:57
  349.6 7.6 convert_bitcast_fusion.3
  365.4 44.8 %all-gather.4 = bf16[1,768,8]{2,0,1:T(2,128)(2,1)} all-gather(bf16[1,48,8]{2,0,1:T(2,128)(2,1)S(1)} %copy.525), channel_id=6, replica_groups=mesh['shard'=4,'dp'=4,'tensor'=2] {'shard','dp'}, dimensions={1}, use_global_device_ids=true | all-gather | bytes 13056 | tf_op jit(solution)/shard_map/all_gather | solution.py:51
  428.3 8.1 gather_fusion
  436.4 5.3 reshape.475
  441.7 7.5 multiply_reduce_fusion.5
  450.0 39.5 %all-gather.7 = bf16[1,768,2]{2,0,1:T(2,128)(2,1)S(1)} all-gather(bf16[1,48,2]{2,0,1:T(2,128)(2,1)S(1)} %copy.526), channel_id=9, replica_groups=mesh['shard'=4,'dp'=4,'tensor'=2] {'shard','dp'}, dimensions={1}, use_global_device_ids=true | all-gather | bytes 3264 | tf_op jit(solution)/shard_map/all_gather | solution.py:52
  490.0 44.6 %all-gather.8 = bf16[1,768,2]{2,0,1:T(2,128)(2,1)S(1)} all-gather(bf16[1,48,2]{2,0,1:T(2,128)(2,1)S(1)} %copy.527), channel_id=10, replica_groups=mesh['shard'=4,'dp'=4,'tensor'=2] {'shard','dp'}, dimensions={1}, use_global_device_ids=true | all-gather | bytes 3264 | tf_op jit(solution)/shard_map/all_gather | solution.py:53
  535.8 43.2 %all-gather.10 = bf16[1,768,384]{2,1,0:T(8,128)(2,1)} all-gather(bf16[1,48,384]{2,1,0:T(8,128)(2,1)S(1)} %copy-done.55), channel_id=12, replica_groups=mesh['shard'=4,'dp'=4,'tensor'=2] {'shard','dp'}, dimensions={1}, use_global_device_ids=true | all-gather | bytes 626688 | tf_op jit(solution)/shard_map/all_gather | solution.py:50
  607.2 18.5 all-reduce.15.cloned.1.call-done
  633.9 10.3 scatter_custom_fusion.1
  655.6 51.9 %all-gather.11 = bf16[1,768,8]{2,0,1:T(2,128)(2,1)S(1)} all-gather(bf16[1,48,8]{2,0,1:T(2,128)(2,1)S(1)} %copy.531), channel_id=13, replica_groups=mesh['shard'=4,'dp'=4,'tensor'=2] {'shard','dp'}, dimensions={1}, use_global_device_ids=true | all-gather | bytes 13056 | tf_op jit(solution)/shard_map/all_gather | solution.py:51
  710.6 5.7 mul.556
  717.1 15.1 scatter_custom_fusion.2
  736.0 5.5 copy.431
  746.2 27.9 fusion.17
  774.1 18.9 all-gather.31.cloned.1.call-done
  793.0 11.6 fusion.14
  817.4 7.6 convert_bitcast_fusion.2
  828.7 15.9 all-to-all-done.5
  861.3 8.2 gather_fusion.2
  869.6 5.4 reshape.487
  875.0 7.4 reduce_sum.427
  888.0 5.4 reshape.499
  893.4 8.3 gather_fusion.1
  901.7 5.4 reshape.483
  907.1 10.8 multiply_reduce_fusion.3
  949.5 18.2 all-reduce.19.cloned.1.call-done
  976.9 5.5 mul.589
  982.4 15.1 scatter_custom_fusion.3
  1005.2 32.3 %all_to_all.40 = bf16[4,2,185,768]{3,1,2,0:T(2,128)(2,1)S(1)} all-to-all(bf16[4,2,185,768]{3,1,2,0:T(2,128)(2,1)S(1)} %copy.450), channel_id=1, replica_groups=mesh['shard'=4,'dp'=4,'tensor'=2] {'shard'}, dimensions={0} | all-to-all | bytes 4546560 | tf_op jit(solution)/shard_map/all_to_all | solution.py:185
  1037.5 11.8 fusion.7
  1055.8 29.1 %all_to_all.41 = bf16[4,2,185,768]{3,1,2,0:T(2,128)(2,1)S(1)} all-to-all(bf16[4,2,185,768]{3,1,2,0:T(2,128)(2,1)S(1)} %copy.452), channel_id=1, replica_groups=mesh['shard'=4,'dp'=4,'tensor'=2] {'shard'}, dimensions={0} | all-to-all | bytes 4546560 | tf_op jit(solution)/shard_map/all_to_all | solution.py:207
  1094.2 8.1 gather_fusion.3
  1102.3 5.4 reshape.492
  1107.6 7.4 reduce_sum.442
  1122.6 11.2 all-reduce.21.cloned.1.call-done
  1177.9 13.3 all-reduce.23.cloned.1.call-done
  1203.6 9.2 bitcast_convert_fusion
  1213.3 9.2 bitcast_convert_fusion.1
  1222.5 9.2 bitcast_convert_fusion.2
  1231.8 9.1 bitcast_convert_fusion.3
  1251.6 67.1 %reduce-scatter.45.cloned.1.call-done = f32[48,8]{1,0:T(8,128)} async-done(((f32[768,8]{1,0:T(8,128)}), f32[48,8]{1,0:T(8,128)}) %reduce-scatter.45.cloned.1.call-update) | async-done | bytes 1552
  1319.6 125.3 %reduce-scatter.53.cloned.1.call-done = f32[48,2]{1,0:T(8,128)} async-done(((f32[768,2]{1,0:T(8,128)}), f32[48,2]{1,0:T(8,128)}) %reduce-scatter.53.cloned.1.call-update) | async-done | bytes 400
  1445.6 124.5 %reduce-scatter.49.cloned.1.call-done = f32[48,2]{1,0:T(8,128)} async-done(((f32[768,2]{1,0:T(8,128)}), f32[48,2]{1,0:T(8,128)}) %reduce-scatter.49.cloned.1.call-update) | async-done | bytes 400
  1570.9 125.2 %reduce-scatter.43.cloned.1.call-done = f32[48,8]{1,0:T(8,128)} async-done(((f32[768,8]{1,0:T(8,128)}), f32[48,8]{1,0:T(8,128)}) %reduce-scatter.43.cloned.1.call-update) | async-done | bytes 1552
  1702.0 119.4 %reduce-scatter.51.cloned.1.call-done = f32[48,2]{1,0:T(8,128)} async-done(((f32[768,2]{1,0:T(8,128)}), f32[48,2]{1,0:T(8,128)}) %reduce-scatter.51.cloned.1.call-update) | async-done | bytes 400
  1822.2 125.1 %reduce-scatter.47.cloned.1.call-done = f32[48,2]{1,0:T(8,128)} async-done(((f32[768,2]{1,0:T(8,128)}), f32[48,2]{1,0:T(8,128)}) %reduce-scatter.47.cloned.1.call-update) | async-done | bytes 400
  1949.3 126.1 %reduce-scatter.33.cloned.1.call-done = f32[48,384]{1,0:T(8,128)} async-done(((f32[768,384]{1,0:T(8,128)}), f32[48,384]{1,0:T(8,128)}) %reduce-scatter.33.cloned.1.call-update) | async-done | bytes 73744 | tf_op jit(solution)/shard_map/reduce_scatter | solution.py:281
  2075.3 127.9 %reduce-scatter.31.cloned.1.call-done = f32[48,384]{1,0:T(8,128)} async-done(((f32[768,384]{1,0:T(8,128)}), f32[48,384]{1,0:T(8,128)}) %reduce-scatter.31.cloned.1.call-update) | async-done | bytes 73744 | tf_op jit(solution)/shard_map/reduce_scatter | solution.py:281
  2204.9 84.8 %reduce-scatter.41.cloned.1.call-done = bf16[2,192,1536]{2,1,0:T(8,128)(2,1)} async-done(((bf16[2,768,1536]{2,1,0:T(8,128)(2,1)}), bf16[2,192,1536]{2,1,0:T(8,128)(2,1)}) %reduce-scatter.41.cloned.1.call-update) | async-done | bytes 1179664 | tf_op jit(solution)/shard_map/reduce_scatter | solution.py:290
  2289.7 88.1 %reduce-scatter.39.cloned.1.call-done = bf16[2,192,1536]{2,1,0:T(8,128)(2,1)} async-done(((bf16[2,768,1536]{2,1,0:T(8,128)(2,1)}), bf16[2,192,1536]{2,1,0:T(8,128)(2,1)}) %reduce-scatter.39.cloned.1.call-update) | async-done | bytes 1179664 | tf_op jit(solution)/shard_map/reduce_scatter | solution.py:290
  2381.9 84.4 %reduce-scatter.37.cloned.1.call-done = bf16[2,192,1536]{2,1,0:T(8,128)(2,1)} async-done(((bf16[2,768,1536]{2,1,0:T(8,128)(2,1)}), bf16[2,192,1536]{2,1,0:T(8,128)(2,1)}) %reduce-scatter.37.cloned.1.call-update) | async-done | bytes 1179664 | tf_op jit(solution)/shard_map/reduce_scatter | solution.py:287
  2466.3 88.1 %reduce-scatter.35.cloned.1.call-done = bf16[2,192,1536]{2,1,0:T(8,128)(2,1)} async-done(((bf16[2,768,1536]{2,1,0:T(8,128)(2,1)}), bf16[2,192,1536]{2,1,0:T(8,128)(2,1)}) %reduce-scatter.35.cloned.1.call-update) | async-done | bytes 1179664 | tf_op jit(solution)/shard_map/reduce_scatter | solution.py:287
  2558.6 136.0 %reduce-scatter.29.cloned.1.call-done = f32[48,3,384]{2,0,1:T(8,128)} async-done(((f32[768,3,384]{2,0,1:T(8,128)}), f32[48,3,384]{2,0,1:T(8,128)}) %reduce-scatter.29.cloned.1.call-update) | async-done | bytes 221200 | tf_op jit(solution)/shard_map/reduce_scatter | solution.py:280
  2694.6 137.7 %reduce-scatter.27.cloned.1.call-done = f32[48,3,384]{2,0,1:T(8,128)} async-done(((f32[768,3,384]{2,0,1:T(8,128)}), f32[48,3,384]{2,0,1:T(8,128)}) %reduce-scatter.27.cloned.1.call-update) | async-done | bytes 221200 | tf_op jit(solution)/shard_map/reduce_scatter | solution.py:280
  (560 shorter events, 349.0 us)
Async XLA Ops:
  8.0 93.6 %copy-start.11 = (bf16[591,768]{1,0:T(8,128)(2,1)S(1)}, bf16[591,768]{1,0:T(8,128)(2,1)}, u32[]{:S(2)}) copy-start(bf16[591,768]{1,0:T(8,128)(2,1)} %param.10) | copy-start | bytes 2723332
  8.0 138.5 %all-gather.21.cloned.1.call-start = ((), (), s32[]{:S(2)}) async-start(), calls=%async_computation.36 | async-start | bytes 1880064 | tf_op jit(solution)/shard_map/all_gather | solution.py:49
  9.8 178.1 %all-reduce.11.cloned.1.call-start = ((), (), s32[]{:S(2)}) async-start(), calls=%async_computation.22 | async-start | bytes 3637248 | tf_op jit(solution)/shard_map/psum | solution.py:83
  58.4 43.9 %copy-start.70 = (bf16[2,48,384]{2,1,0:T(8,128)(2,1)S(1)}, bf16[2,48,384]{2,1,0:T(8,128)(2,1)}, u32[]{:S(2)}) copy-start(bf16[2,48,384]{2,1,0:T(8,128)(2,1)} %param.13) | copy-start | bytes 221188
  101.2 49.6 %copy-start.74 = (f32[768]{0:T(1024)}, f32[768]{0:T(1024)S(1)}, u32[]{:S(2)}) copy-start(f32[768]{0:T(1024)S(1)} %get-tuple-element.31) | copy-start | bytes 9220
  101.2 88.8 %copy-start.76 = (f32[768]{0:T(1024)}, f32[768]{0:T(1024)S(1)}, u32[]{:S(2)}) copy-start(f32[768]{0:T(1024)S(1)} %get-tuple-element.30) | copy-start | bytes 9220
  101.6 49.2 %copy-start.109 = (f32[768]{0:T(1024)}, f32[768]{0:T(1024)S(1)}, u32[]{:S(2)}) copy-start(f32[768]{0:T(1024)S(1)} %get-tuple-element.33) | copy-start | bytes 9220
  101.9 49.0 %copy-start.58 = (f32[591]{0:T(1024)}, f32[591]{0:T(1024)S(1)}, u32[]{:S(2)}) copy-start(f32[591]{0:T(1024)S(1)} %broadcast_multiply_fusion.5) | copy-start | bytes 7096
  102.3 48.6 %copy-start.95 = (f32[591]{0:T(1024)}, f32[591]{0:T(1024)S(1)}, u32[]{:S(2)}) copy-start(f32[591]{0:T(1024)S(1)} %fusion.99) | copy-start | bytes 7096
  102.3 48.5 %copy-start.91 = (f32[591]{0:T(1024)}, f32[591]{0:T(1024)S(1)}, u32[]{:S(2)}) copy-start(f32[591]{0:T(1024)S(1)} %fusion.205) | copy-start | bytes 7096
  146.6 22.6 copy-start.33
  171.1 88.7 %all-gather.23.cloned.1.call-start = ((), (), s32[]{:S(2)}) async-start(), calls=%async_computation.37 | async-start | bytes 5898240 | tf_op jit(solution)/shard_map/all_gather | solution.py:56
  175.3 243.0 %copy-start.88 = (s32[591,2]{0,1:T(2,128)}, s32[591,2]{0,1:T(2,128)S(1)}, u32[]{:S(2)}) copy-start(s32[591,2]{0,1:T(2,128)S(1)} %get-tuple-element.65) | copy-start | bytes 14188
  191.2 226.7 %copy-start.19 = (bf16[591,768]{1,0:T(8,128)(2,1)}, bf16[591,768]{1,0:T(8,128)(2,1)S(1)}, u32[]{:S(2)}) copy-start(bf16[591,768]{1,0:T(8,128)(2,1)S(1)} %add_convert_fusion.3) | copy-start | bytes 2723332
  212.4 32.2 %all-to-all-start = ((bf16[4,2,185,768]{3,1,2,0:T(2,128)(2,1)}), bf16[4,2,185,768]{3,1,2,0:T(2,128)(2,1)}, u32[]{:S(2)}, u32[]{:S(2)}) async-start(bf16[4,2,185,768]{3,1,2,0:T(2,128)(2,1)} %copy.406), calls=%async_computation | async-start | bytes 4546560 | tf_op jit(solution)/shard_map/all_to_all | solution.py:99
  217.1 132.5 %all-gather.25.cloned.1.call-start = ((), (), s32[]{:S(2)}) async-start(), calls=%async_computation.38 | async-start | bytes 5898240 | tf_op jit(solution)/shard_map/all_gather | solution.py:57
  360.9 58.2 %all-to-all-start.1 = ((bf16[4,2,185,768]{3,1,2,0:T(2,128)(2,1)}), bf16[4,2,185,768]{3,1,2,0:T(2,128)(2,1)S(1)}, u32[]{:S(2)}, u32[]{:S(2)}) async-start(bf16[4,2,185,768]{3,1,2,0:T(2,128)(2,1)} %copy.408), calls=%async_computation.1 | async-start | bytes 4546560 | tf_op jit(solution)/shard_map/all_to_all | solution.py:113
  364.7 214.2 %all-reduce.13.cloned.1.call-start = ((), (), s32[]{:S(2)}) async-start(), calls=%async_computation.23 | async-start | bytes 1818624 | tf_op jit(solution)/shard_map/psum | solution.py:118
  419.1 22.6 copy-start.38
  441.7 48.1 %copy-start.115 = (bf16[1,48,2]{1,2,0:T(2,128)(2,1)S(1)}, bf16[1,48,2]{1,2,0:T(2,128)(2,1)}, u32[]{:S(2)}) copy-start(bf16[1,48,2]{1,2,0:T(2,128)(2,1)} %get-tuple-element.76) | copy-start | bytes 580
  449.2 86.6 %copy-start.55 = (bf16[1,48,384]{2,1,0:T(8,128)(2,1)S(1)}, bf16[1,48,384]{2,1,0:T(8,128)(2,1)}, u32[]{:S(2)}) copy-start(bf16[1,48,384]{2,1,0:T(8,128)(2,1)} %get-tuple-element.62) | copy-start | bytes 110596
  449.2 132.2 %all-gather.27.cloned.1.call-start = ((), (), s32[]{:S(2)}) async-start(), calls=%async_computation.39 | async-start | bytes 1880064 | tf_op jit(solution)/shard_map/all_gather | solution.py:49
  449.8 175.9 %all-reduce.15.cloned.1.call-start = ((), (), s32[]{:S(2)}) async-start(), calls=%async_computation.24 | async-start | bytes 3637248 | tf_op jit(solution)/shard_map/psum | solution.py:83
  535.3 46.8 %copy-start.78 = (f32[768]{0:T(1024)}, f32[768]{0:T(1024)S(1)}, u32[]{:S(2)}) copy-start(f32[768]{0:T(1024)S(1)} %get-tuple-element.27) | copy-start | bytes 9220
  535.3 92.5 %copy-start.80 = (f32[768]{0:T(1024)}, f32[768]{0:T(1024)S(1)}, u32[]{:S(2)}) copy-start(f32[768]{0:T(1024)S(1)} %get-tuple-element.26) | copy-start | bytes 9220
  535.7 46.4 %copy-start.111 = (f32[768]{0:T(1024)}, f32[768]{0:T(1024)S(1)}, u32[]{:S(2)}) copy-start(f32[768]{0:T(1024)S(1)} %get-tuple-element.29) | copy-start | bytes 9220
  581.0 44.7 %copy-start.4 = (f32[591,768]{1,0:T(8,128)}, f32[591,768]{1,0:T(8,128)S(1)}, u32[]{:S(2)}) copy-start(f32[591,768]{1,0:T(8,128)S(1)} %get-tuple-element.45) | copy-start | bytes 5446660
  606.6 139.6 %all-gather.29.cloned.1.call-start = ((), (), s32[]{:S(2)}) async-start(), calls=%async_computation.40 | async-start | bytes 5898240 | tf_op jit(solution)/shard_map/all_gather | solution.py:56
  629.0 87.3 %copy-start.20 = (bf16[591,768]{1,0:T(8,128)(2,1)}, bf16[591,768]{1,0:T(8,128)(2,1)S(1)}, u32[]{:S(2)}) copy-start(bf16[591,768]{1,0:T(8,128)(2,1)S(1)} %add_convert_fusion.1) | copy-start | bytes 2723332
  650.2 57.6 %copy-start.21 = (bf16[591,768]{1,0:T(8,128)(2,1)S(1)}, bf16[591,768]{1,0:T(8,128)(2,1)}, u32[]{:S(2)}) copy-start(bf16[591,768]{1,0:T(8,128)(2,1)} %param.19) | copy-start | bytes 2723332
  650.2 91.3 %all-to-all-start.2 = ((bf16[4,2,185,768]{3,1,2,0:T(2,128)(2,1)}), bf16[4,2,185,768]{3,1,2,0:T(2,128)(2,1)}, u32[]{:S(2)}, u32[]{:S(2)}) async-start(bf16[4,2,185,768]{3,1,2,0:T(2,128)(2,1)} %copy.425), calls=%async_computation.2 | async-start | bytes 4546560 | tf_op jit(solution)/shard_map/all_to_all | solution.py:99
  654.8 138.2 %all-gather.31.cloned.1.call-start = ((), (), s32[]{:S(2)}) async-start(), calls=%async_computation.41 | async-start | bytes 5898240 | tf_op jit(solution)/shard_map/all_gather | solution.py:57
  741.4 51.6 %all-to-all-start.4 = ((bf16[4,2,185,768]{3,1,2,0:T(2,128)(2,1)}), bf16[4,2,185,768]{3,1,2,0:T(2,128)(2,1)}, u32[]{:S(2)}, u32[]{:S(2)}) async-start(bf16[4,2,185,768]{3,1,2,0:T(2,128)(2,1)} %copy.431), calls=%async_computation.4 | async-start | bytes 4546560 | tf_op jit(solution)/shard_map/all_to_all | solution.py:185
  812.9 31.7 %all-to-all-start.5 = ((bf16[4,2,185,768]{3,1,2,0:T(2,128)(2,1)}), bf16[4,2,185,768]{3,1,2,0:T(2,128)(2,1)}, u32[]{:S(2)}, u32[]{:S(2)}) async-start(bf16[4,2,185,768]{3,1,2,0:T(2,128)(2,1)} %copy.433), calls=%async_computation.5 | async-start | bytes 4546560 | tf_op jit(solution)/shard_map/all_to_all | solution.py:207
  844.6 37.9 %all-to-all-start.3 = ((bf16[4,2,185,768]{3,1,2,0:T(2,128)(2,1)}), bf16[4,2,185,768]{3,1,2,0:T(2,128)(2,1)}, u32[]{:S(2)}, u32[]{:S(2)}) async-start(bf16[4,2,185,768]{3,1,2,0:T(2,128)(2,1)} %copy.427), calls=%async_computation.3 | async-start | bytes 4546560 | tf_op jit(solution)/shard_map/all_to_all | solution.py:113
  849.1 71.5 %all-reduce.17.cloned.1.call-start = ((), (), s32[]{:S(2)}) async-start(), calls=%async_computation.25 | async-start | bytes 1818624 | tf_op jit(solution)/shard_map/psum | solution.py:215
  882.4 85.3 %all-reduce.19.cloned.1.call-start = ((), (), s32[]{:S(2)}) async-start(), calls=%async_computation.26 | async-start | bytes 1818624 | tf_op jit(solution)/shard_map/psum | solution.py:273
  946.8 20.8 copy-start.5
  946.8 20.8 copy-start.61
  946.8 20.8 copy-start.79
  949.2 21.1 copy-start.100
  949.2 21.1 copy-start.94
  949.2 184.6 %all-reduce.21.cloned.1.call-start = ((), (), s32[]{:S(2)}) async-start(), calls=%async_computation.27 | async-start | bytes 1818624 | tf_op jit(solution)/shard_map/psum | solution.py:215
  1005.2 44.2 %slice-start = ((s8[4718592]{0:T(1024)(128)(4,1)}), s8[4194304]{0:T(1024)(128)(4,1)S(1)}, s32[]{:S(2)}) async-start(s8[4718592]{0:T(1024)(128)(4,1)} %bitcast.452), calls=%async_computation.49 | async-start | bytes 8388608
  1115.0 76.1 %all-reduce.23.cloned.1.call-start = ((), (), s32[]{:S(2)}) async-start(), calls=%async_computation.48 | async-start | bytes 3637248 | tf_op jit(solution)/shard_map/psum | solution.py:118
  1169.0 22.2 copy-start.12
  1169.0 22.2 copy-start.59
  1169.0 22.2 copy-start.75
  1169.0 149.8 %reduce-scatter.45.cloned.1.call-start = ((), (), s32[]{:S(2)}) async-start(), calls=%async_computation.43 | async-start | bytes 417792
  1172.4 272.4 %reduce-scatter.53.cloned.1.call-start = ((), (), s32[]{:S(2)}) async-start(), calls=%async_computation.47 | async-start | bytes 417792
  1173.5 19.6 copy-start.92
  1173.5 396.6 %reduce-scatter.49.cloned.1.call-start = ((), (), s32[]{:S(2)}) async-start(), calls=%async_computation.45 | async-start | bytes 417792
  1174.6 521.6 %reduce-scatter.43.cloned.1.call-start = ((), (), s32[]{:S(2)}) async-start(), calls=%async_computation.42 | async-start | bytes 417792
  1177.8 643.6 %reduce-scatter.51.cloned.1.call-start = ((), (), s32[]{:S(2)}) async-start(), calls=%async_computation.46 | async-start | bytes 417792
  1195.2 752.1 %reduce-scatter.47.cloned.1.call-start = ((), (), s32[]{:S(2)}) async-start(), calls=%async_computation.44 | async-start | bytes 417792
  1196.3 879.1 %reduce-scatter.33.cloned.1.call-start = ((), (), s32[]{:S(2)}) async-start(), calls=%async_computation.31 | async-start | bytes 1253376 | tf_op jit(solution)/shard_map/reduce_scatter | solution.py:281
  1200.2 1003.1 %reduce-scatter.31.cloned.1.call-start = ((), (), s32[]{:S(2)}) async-start(), calls=%async_computation.30 | async-start | bytes 1253376 | tf_op jit(solution)/shard_map/reduce_scatter | solution.py:281
  1203.6 1086.1 %reduce-scatter.41.cloned.1.call-start = ((), (), s32[]{:S(2)}) async-start(), calls=%async_computation.35 | async-start | bytes 5898240 | tf_op jit(solution)/shard_map/reduce_scatter | solution.py:290
  1212.8 1165.0 %reduce-scatter.39.cloned.1.call-start = ((), (), s32[]{:S(2)}) async-start(), calls=%async_computation.34 | async-start | bytes 5898240 | tf_op jit(solution)/shard_map/reduce_scatter | solution.py:290
  1222.5 1243.8 %reduce-scatter.37.cloned.1.call-start = ((), (), s32[]{:S(2)}) async-start(), calls=%async_computation.33 | async-start | bytes 5898240 | tf_op jit(solution)/shard_map/reduce_scatter | solution.py:287
  1231.7 1322.7 %reduce-scatter.35.cloned.1.call-start = ((), (), s32[]{:S(2)}) async-start(), calls=%async_computation.32 | async-start | bytes 5898240 | tf_op jit(solution)/shard_map/reduce_scatter | solution.py:287
  1240.9 1453.6 %reduce-scatter.29.cloned.1.call-start = ((), (), s32[]{:S(2)}) async-start(), calls=%async_computation.29 | async-start | bytes 3760128 | tf_op jit(solution)/shard_map/reduce_scatter | solution.py:280
  1246.6 1585.7 %reduce-scatter.27.cloned.1.call-start = ((), (), s32[]{:S(2)}) async-start(), calls=%async_computation.28 | async-start | bytes 3760128 | tf_op jit(solution)/shard_map/reduce_scatter | solution.py:280
  1251.6 446.0 %copy-start.8 = (f32[591,768]{1,0:T(8,128)S(1)}, f32[591,768]{1,0:T(8,128)}, u32[]{:S(2)}) copy-start(f32[591,768]{1,0:T(8,128)} %copy-done.6) | copy-start | bytes 5446660
  (92 other events, 483.8 us)
Sparse Core Ops, SparseCore 0:
  12.3 62.9 all-gather.20
  171.2 16.6 all-reduce.10
  449.3 15.7 all-reduce.12
  468.9 62.0 all-gather.26
  606.7 18.9 all-reduce.14
  882.5 18.0 all-reduce.16
  949.3 18.2 all-reduce.18
  1115.1 18.5 all-reduce.20
  1169.1 22.0 all-reduce.22
  1196.2 122.4 reduce-scatter.44
  1324.1 120.6 reduce-scatter.52
  1449.3 120.7 reduce-scatter.48
  1575.5 120.6 reduce-scatter.42
  1700.7 120.6 reduce-scatter.50
  1826.6 120.6 reduce-scatter.46
  1951.9 123.3 reduce-scatter.32
  2079.9 123.2 reduce-scatter.30
  2205.4 84.2 reduce-scatter.40
  2292.0 85.7 reduce-scatter.38
  2380.5 85.7 reduce-scatter.36
  2468.6 85.7 reduce-scatter.34
  2559.6 134.9 reduce-scatter.28
  2699.7 132.5 reduce-scatter.26
Sparse Core Ops, SparseCore 1:
  174.7 85.1 all-gather.22
  261.9 87.7 all-gather.24
  608.7 95.0 all-gather.28
  705.5 87.5 all-gather.30
where the time goes:
time: 2850 us; the launch traced here: 2840 us
  waiting for transfers between devices  1770 us (62%)
  blocking collectives  422 us (15%)
  local copies, waits for them, and re-layouts  274 us (10%)
  matrix products  205 us (7%)
  other arithmetic  125 us (4%)
  starting transfers between devices  29.6 us (1%)
    unnamed x33, waiting for transfers between devices  688 us
    reduce_scatter x2, waiting for transfers between devices, on_device(): lax.psum_scatter(qkv_grad, ('shard', 'dp'), scatter_dimension=0, tiled=True)  274 us
    reduce_scatter x2, waiting for transfers between devices, on_device(): lax.psum_scatter(out_proj_grad, ('shard', 'dp'), scatter_dimension=0, til...  254 us
    reduce_scatter x2, waiting for transfers between devices, on_device(): lax.psum_scatter(down_grad.astype(jnp.bfloat16), 'dp', scatter_dimension=...  173 us
    reduce_scatter x2, waiting for transfers between devices, on_device(): lax.psum_scatter(in_grad.astype(jnp.bfloat16), 'dp', scatter_dimension=1,...  173 us
    all_gather x2, blocking collectives, on_device(): lax.all_gather(w_router[depth], ('shard', 'dp'), axis=0, tiled=True)  96.7 us
    all_gather x2, blocking collectives, on_device(): lax.all_gather(w_out[depth], ('shard', 'dp'), axis=0, tiled=True)  86.8 us
    all_gather x2, blocking collectives, on_device(): lax.all_gather(ln_gain[depth], ('shard', 'dp'), axis=0, tiled=True)  86.3 us
  transfers between devices with their start and end apart: 33, of which 24 were waited for; matrix products, arithmetic and copies ran while one was open for 12% of the time, Pallas kernels for 0%

commit v1 on v0

v1 whole, which is shorter than its diff:
```python
import functools

import jax
import jax.numpy as jnp
from jax import lax
from jax.experimental import pallas as pl
from jax.experimental.pallas import tpu as pltpu
from jax.sharding import PartitionSpec as P

D = 768
HEAD_DIM = 64
SEQ = 197
LAYERS = 2
LANES = 128
F32 = jnp.float32
BF16 = jnp.bfloat16
NN = (((1,), (0,)), ((), ()))
NT = (((1,), (1,)), ((), ()))
TN = (((0,), (0,)), ((), ()))


def round_up(value, step):
    return -(-value // step) * step


def mm(left, right, dims=NN):
    return lax.dot_general(left, right, dims, preferred_element_type=F32)


def split_low(values):
    high = values.astype(BF16)
    return high, (values - high.astype(F32)).astype(BF16)


def norm_parts(values):
    centred = values - jnp.mean(values, axis=-1, keepdims=True)
    rstd = lax.rsqrt(jnp.mean(centred * centred, axis=-1, keepdims=True) + 1e-06)
    return centred * rstd, rstd


def norm_back(unit, rstd, gain, grad):
    scaled = grad * gain
    return rstd * (
        scaled
        - jnp.mean(scaled, axis=-1, keepdims=True)
        - unit * jnp.mean(scaled * unit, axis=-1, keepdims=True)
    )


def params(mib=48, **more):
    return pltpu.CompilerParams(vmem_limit_bytes=mib * 1024 * 1024, **more)


def head_mask(half):
    lane = lax.broadcasted_iota(jnp.int32, (1, LANES), 1)
    return (lane // HEAD_DIM) == half


def masked(values, keep):
    return jnp.where(keep, values, jnp.zeros_like(values))


def head_probs(query, keys, key_ok):
    scores = mm(query, keys, NT) * (HEAD_DIM**-0.5)
    scores = jnp.where(key_ok, scores, -1e30)
    exponent = jnp.exp(scores - jnp.max(scores, axis=-1, keepdims=True))
    return exponent / jnp.sum(exponent, axis=-1, keepdims=True)


def attn_fwd_kernel(x_ref, w_ref, wo_ref, g_ref, b_ref, normed_ref, packed_ref, heads_ref, part_ref):
    rows = x_ref.shape[0]
    width = wo_ref.shape[1]
    unit, _ = norm_parts(x_ref[...])
    normed = (unit * g_ref[...] + b_ref[...]).astype(BF16)
    normed_ref[...] = normed
    packed_ref[...] = mm(normed, w_ref[...]).astype(BF16)
    key_ok = lax.broadcasted_iota(jnp.int32, (1, rows), 1) < SEQ
    for pair in range(width // LANES):
        low = pair * LANES
        query = packed_ref[:, low : low + LANES]
        keys = packed_ref[:, width + low : width + low + LANES]
        vals = packed_ref[:, 2 * width + low : 2 * width + low + LANES]
        outs = []
        for half in range(2):
            probs = head_probs(masked(query, head_mask(half)), keys, key_ok).astype(BF16)
            outs.append(mm(probs, vals))
        heads_ref[:, low : low + LANES] = jnp.where(head_mask(0), outs[0], outs[1]).astype(BF16)
    part_ref[...] = mm(heads_ref[...], wo_ref[...], NT).astype(BF16)


def weight_specs(width):
    return [
        pl.BlockSpec((D, 3 * width), lambda i: (0, 0)),
        pl.BlockSpec((D, width), lambda i: (0, 3)),
    ]


def rows_spec(rows, cols):
    return pl.BlockSpec((rows, cols), lambda i: (i, 0))


def whole_spec(shape):
    return pl.BlockSpec(shape, lambda i: (0,) * len(shape))


def attn_fwd(stream, gathered, gain, shift, images, width):
    tok = stream.shape[0]
    rows = tok // images
    return pl.pallas_call(
        attn_fwd_kernel,
        grid=(images,),
        in_specs=[rows_spec(rows, D)] + weight_specs(width) + [whole_spec((1, D))] * 2,
        out_specs=[
            rows_spec(rows, D),
            rows_spec(rows, 3 * width),
            rows_spec(rows, width),
            rows_spec(rows, D),
        ],
        out_shape=[
            jax.ShapeDtypeStruct((tok, D), BF16),
            jax.ShapeDtypeStruct((tok, 3 * width), BF16),
            jax.ShapeDtypeStruct((tok, width), BF16),
            jax.ShapeDtypeStruct((tok, D), BF16),
        ],
        compiler_params=params(),
        name="attn_fwd",
    )(stream, gathered, gathered, gain, shift)


def slot_rows(dest_row, start, count, k):
    at = lax.broadcasted_iota(jnp.int32, (count, 1), 0) + start
    return jnp.where(at == dest_row[k : k + 1, :], 1.0, 0.0).astype(BF16)


def slot_cols(dest_col, slots, k):
    at = lax.broadcasted_iota(jnp.int32, (1, slots), 1)
    return jnp.where(at == dest_col[:, k : k + 1], 1.0, 0.0).astype(BF16)


def expert_lane(ids, k):
    lane = lax.broadcasted_iota(jnp.int32, (1, LANES), 1)
    return jnp.where(lane == ids[:, k : k + 1], 1.0, 0.0)


def mid_kernel(
    x_ref, pa_ref, pb_ref, g_ref, b_ref, small_ref, ids_ref, dest_ref,
    middle_ref, act_ref, gates_ref, out_ref,
):
    middle = x_ref[...] + (pa_ref[...].astype(F32) + pb_ref[...].astype(F32))
    middle_ref[...] = middle
    unit, _ = norm_parts(middle)
    act_ref[...] = (unit * g_ref[...] + b_ref[...]).astype(BF16)
    logits = mm(act_ref[...], small_ref[...])
    first = jnp.sum(expert_lane(ids_ref, 0) * logits, axis=-1, keepdims=True)
    second = jnp.sum(expert_lane(ids_ref, 1) * logits, axis=-1, keepdims=True)
    top = jnp.maximum(first, second)
    first, second = jnp.exp(first - top), jnp.exp(second - top)
    total = first + second
    lane = lax.broadcasted_iota(jnp.int32, (1, LANES), 1)
    gates_ref[...] = jnp.where(lane == 0, first / total, jnp.where(lane == 1, second / total, 0.0))
    slots = out_ref.shape[0]
    chunk = slots // 4
    for start in range(0, slots, chunk):
        pick = slot_rows(dest_ref, start, chunk, 0) + slot_rows(dest_ref, start, chunk, 1)
        out_ref[start : start + chunk, :] = mm(pick, act_ref[...]).astype(BF16)


def mid_fwd(stream, own, peer, gain, shift, gathered, ids, dest_row, slots, width):
    tok = stream.shape[0]
    full = whole_spec((tok, D))
    return pl.pallas_call(
        mid_kernel,
        grid=(1,),
        in_specs=[full, full, full, whole_spec((1, D)), whole_spec((1, D))]
        + [pl.BlockSpec((D, LANES), lambda i: (0, 4 * width // LANES))]
        + [whole_spec((tok, 2)), whole_spec((2, tok))],
        out_specs=[full, full, whole_spec((tok, LANES)), whole_spec((slots, D))],
        out_shape=[
            jax.ShapeDtypeStruct((tok, D), F32),
            jax.ShapeDtypeStruct((tok, D), BF16),
            jax.ShapeDtypeStruct((tok, LANES), F32),
            jax.ShapeDtypeStruct((slots, D), BF16),
        ],
        compiler_params=params(),
        name="mid_fwd",
    )(stream, own, peer, gain, shift, gathered, ids, dest_row)


def ffn_fwd_kernel(x_ref, wi_ref, wo_ref, y_ref, act_ref, slope_ref, acc_ref):
    rows, chunk = acc_ref.shape[0], wi_ref.shape[2]
    x = x_ref[...].reshape(rows, D)
    pre = mm(x, wi_ref[0])
    cdf = 0.5 * (1.0 + lax.erf(pre * (0.5**0.5)))
    act = (pre * cdf).astype(BF16)
    slope = cdf + pre * (jnp.exp(-0.5 * pre * pre) * 0.3989422804014327)
    act_ref[...] = act.reshape(act_ref.shape)
    slope_ref[...] = slope.astype(BF16).reshape(slope_ref.shape)
    part = mm(act, wo_ref[0], NT)
    step = pl.program_id(1)

    @pl.when(step == 0)
    def _():
        acc_ref[...] = part

    @pl.when(step > 0)
    def _():
        acc_ref[...] += part

    @pl.when(step == pl.num_programs(1) - 1)
    def _():
        y_ref[...] = acc_ref[...].astype(BF16).reshape(y_ref.shape)


def ffn_specs(shards, cap, chunk):
    token = pl.BlockSpec((shards, 1, cap, D), lambda e, f: (0, e, 0, 0))
    weight = pl.BlockSpec((1, D, chunk), lambda e, f: (e, 0, f))
    hidden = pl.BlockSpec((shards, 1, cap, chunk), lambda e, f: (0, e, 0, f))
    return token, weight, hidden


def ffn_fwd(received, weight_in, weight_down):
    shards, exp_dev, cap, _ = received.shape
    hidden_dev = weight_in.shape[2]
    chunk = 512
    token, weight, hidden = ffn_specs(shards, cap, chunk)
    hidden_shape = jax.ShapeDtypeStruct((shards, exp_dev, cap, hidden_dev), BF16)
    return pl.pallas_call(
        ffn_fwd_kernel,
        grid=(exp_dev, hidden_dev // chunk),
        in_specs=[token, weight, weight],
        out_specs=[token, hidden, hidden],
        out_shape=[jax.ShapeDtypeStruct(received.shape, BF16), hidden_shape, hidden_shape],
        scratch_shapes=[pltpu.VMEM((shards * cap, D), F32)],
        compiler_params=params(),
        name="ffn_fwd",
    )(received, weight_in, weight_down)


def ffn_bwd_kernel(
    xa_ref, xb_ref, da_ref, db_ref, acta_ref, actb_ref, slopea_ref, slopeb_ref, wi_ref, wo_ref,
    dxa_ref, dxb_ref, gi_ref, go_ref, acc_ref,
):
    rows = acc_ref.shape[0]
    half = rows // 2
    chunk = wi_ref.shape[2]

    def both(first, second, cols):
        return jnp.concatenate(
            [first[...].reshape(half, cols), second[...].reshape(half, cols)], axis=0
        )

    x = both(xa_ref, xb_ref, D)
    dy = both(da_ref, db_ref, D)
    act = both(acta_ref, actb_ref, chunk)
    slope = both(slopea_ref, slopeb_ref, chunk)
    dpre = (mm(dy, wo_ref[0]) * slope.astype(F32)).astype(BF16)
    go_ref[0] = mm(dy, act, TN).astype(BF16)
    gi_ref[0] = mm(x, dpre, TN).astype(BF16)
    part = mm(dpre, wi_ref[0], NT)
    step = pl.program_id(1)

    @pl.when(step == 0)
    def _():
        acc_ref[...] = part

    @pl.when(step > 0)
    def _():
        acc_ref[...] += part

    @pl.when(step == pl.num_programs(1) - 1)
    def _():
        dxa_ref[...] = acc_ref[:half].astype(BF16).reshape(dxa_ref.shape)
        dxb_ref[...] = acc_ref[half:].astype(BF16).reshape(dxb_ref.shape)


def ffn_bwd(received, grad_in, act, slope, weight_in, weight_down):
    shards, exp_dev, cap, _ = received[0].shape
    hidden_dev = weight_in.shape[2]
    chunk = 512
    token, weight, hidden = ffn_specs(shards, cap, chunk)
    grad_shape = jax.ShapeDtypeStruct(weight_in.shape, BF16)
    row_shape = jax.ShapeDtypeStruct(received[0].shape, BF16)
    return pl.pallas_call(
        ffn_bwd_kernel,
        grid=(exp_dev, hidden_dev // chunk),
        in_specs=[token] * 4 + [hidden] * 4 + [weight, weight],
        out_specs=[token, token, weight, weight],
        out_shape=[row_shape, row_shape, grad_shape, grad_shape],
        scratch_shapes=[pltpu.VMEM((2 * shards * cap, D), F32)],
        compiler_params=params(),
        name="ffn_bwd",
    )(*received, *grad_in, *act, *slope, weight_in, weight_down)


def combine_kernel(y_ref, dest_ref, gates_ref, taken_ref, part_ref):
    slots = y_ref.shape[0]
    total = None
    for k in range(2):
        picked = mm(slot_cols(dest_ref, slots, k), y_ref[...])
        taken_ref[k] = picked.astype(BF16)
        term = gates_ref[:, k : k + 1] * picked
        total = term if total is None else total + term
    part_ref[...] = total.astype(BF16)


def combine_fwd(returned, dest_col, gates, images):
    slots = returned.shape[0]
    tok = dest_col.shape[0]
    rows = tok // images
    return pl.pallas_call(
        combine_kernel,
        grid=(images,),
        in_specs=[whole_spec((slots, D)), rows_spec(rows, 2), rows_spec(rows, LANES)],
        out_specs=[pl.BlockSpec((2, rows, D), lambda i: (0, i, 0)), rows_spec(rows, D)],
        out_shape=[
            jax.ShapeDtypeStruct((2, tok, D), BF16),
            jax.ShapeDtypeStruct((tok, D), BF16),
        ],
        compiler_params=params(),
        name="combine_fwd",
    )(returned, dest_col, gates)


def spread_kernel(grad_ref, gates_ref, taken_ref, dest_ref, out_ref, pgate_ref):
    grad = grad_ref[...]
    lane = lax.broadcasted_iota(jnp.int32, (1, LANES), 1)
    dys, dots = [], []
    for k in range(2):
        dys.append((gates_ref[:, k : k + 1] * grad).astype(BF16))
        dots.append(jnp.sum(grad * taken_ref[k].astype(F32), axis=-1, keepdims=True))
    pgate_ref[...] = jnp.where(lane == 0, dots[0], jnp.where(lane == 1, dots[1], 0.0)).astype(BF16)
    slots = out_ref.shape[0]
    chunk = slots // 4
    for start in range(0, slots, chunk):
        total = mm(slot_rows(dest_ref, start, chunk, 0), dys[0])
        total = total + mm(slot_rows(dest_ref, start, chunk, 1), dys[1])
        out_ref[start : start + chunk, :] = total.astype(BF16)


def spread_bwd(grad, gates, taken, dest_row, slots):
    tok = grad.shape[0]
    return pl.pallas_call(
        spread_kernel,
        grid=(1,),
        in_specs=[
            whole_spec((tok, D)),
            whole_spec((tok, LANES)),
            whole_spec((2, tok, D)),
            whole_spec((2, tok)),
        ],
        out_specs=[whole_spec((slots, D)), whole_spec((tok, LANES))],
        out_shape=[
            jax.ShapeDtypeStruct((slots, D), BF16),
            jax.ShapeDtypeStruct((tok, LANES), BF16),
        ],
        compiler_params=params(),
        name="spread_bwd",
    )(grad, gates, taken, dest_row)


def gather_kernel(rows_ref, dest_ref, pgate_ref, out_ref):
    slots = rows_ref.shape[0]
    pick = slot_cols(dest_ref, slots, 0) + slot_cols(dest_ref, slots, 1)
    out_ref[:, :D] = mm(pick, rows_ref[...]).astype(BF16)
    out_ref[:, D:] = pgate_ref[...]


def gather_bwd(rows_back, dest_col, pgate, images):
    slots = rows_back.shape[0]
    tok = dest_col.shape[0]
    rows = tok // images
    return pl.pallas_call(
        gather_kernel,
        grid=(images,),
        in_specs=[whole_spec((slots, D)), rows_spec(rows, 2), rows_spec(rows, LANES)],
        out_specs=rows_spec(rows, D + LANES),
        out_shape=jax.ShapeDtypeStruct((tok, D + LANES), BF16),
        compiler_params=params(),
        name="gather_bwd",
    )(rows_back, dest_col, pgate)


def attn_bwd_kernel(
    own_ref, peer_ref, middle_ref, act_ref, gates_ref, ids_ref, grad_ref, normed_ref, packed_ref,
    heads_ref, w_ref, wo_ref, small_ref, g_ref,
    mgrad_ref, pnorm_ref, qkvg_ref, outg_ref, routerg_ref, lng_ref, dpacked_ref,
):
    rows = middle_ref.shape[0]
    width = wo_ref.shape[1]

    @pl.when(pl.program_id(0) == 0)
    def _():
        qkvg_ref[...] = jnp.zeros_like(qkvg_ref)
        outg_ref[...] = jnp.zeros_like(outg_ref)
        routerg_ref[...] = jnp.zeros_like(routerg_ref)
        lng_ref[...] = jnp.zeros_like(lng_ref)

    both = own_ref[...].astype(F32) + peer_ref[...].astype(F32)
    act_grad, dgate = both[:, :D], both[:, D:]
    gates = gates_ref[...]
    chosen = gates * (dgate - jnp.sum(gates * dgate, axis=-1, keepdims=True))
    dlogit = expert_lane(ids_ref, 0) * chosen[:, 0:1] + expert_lane(ids_ref, 1) * chosen[:, 1:2]
    high, low = split_low(dlogit)
    act = act_ref[...]
    routerg_ref[...] += mm(act, high, TN) + mm(act, low, TN)
    act_grad = act_grad + mm(high, small_ref[...], NT) + mm(low, small_ref[...], NT)
    unit, rstd = norm_parts(middle_ref[...])
    lng_ref[0:1, :] += jnp.sum(act_grad * unit, axis=0, keepdims=True)
    lng_ref[1:2, :] += jnp.sum(act_grad, axis=0, keepdims=True)
    mgrad = grad_ref[...] + norm_back(unit, rstd, g_ref[...], act_grad)
    mgrad_ref[...] = mgrad
    attn_grad = mgrad.astype(BF16)
    outg_ref[...] += mm(attn_grad, heads_ref[...], TN)
    dheads = mm(attn_grad, wo_ref[...]).astype(BF16)
    key_ok = lax.broadcasted_iota(jnp.int32, (1, rows), 1) < SEQ
    scale = HEAD_DIM**-0.5
    for pair in range(width // LANES):
        at = pair * LANES
        query = packed_ref[:, at : at + LANES]
        keys = packed_ref[:, width + at : width + at + LANES]
        vals = packed_ref[:, 2 * width + at : 2 * width + at + LANES]
        dhead = dheads[:, at : at + LANES]
        terms = []
        for half in range(2):
            keep = head_mask(half)
            probs = head_probs(masked(query, keep), keys, key_ok)
            dprobs = mm(masked(dhead, keep), vals, NT)
            dscores = probs * (dprobs - jnp.sum(probs * dprobs, axis=-1, keepdims=True))
            dscores = dscores.astype(BF16)
            terms.append(
                (
                    mm(dscores, keys) * scale,
                    mm(dscores, query, TN) * scale,
                    mm(probs.astype(BF16), dhead, TN),
                )
            )
        for part in range(3):
            start = part * width + at
            dpacked_ref[:, start : start + LANES] = jnp.where(
                head_mask(0), terms[0][part], terms[1][part]
            ).astype(BF16)
    qkvg_ref[...] += mm(normed_ref[...], dpacked_ref[...], TN)
    pnorm_ref[...] = mm(dpacked_ref[...], w_ref[...], NT).astype(BF16)


def attn_bwd(own, peer, saved, grad, gathered, gain, ids, images, width):
    middle, act_in, gates, normed, packed, heads = saved
    tok = middle.shape[0]
    rows = tok // images
    return pl.pallas_call(
        attn_bwd_kernel,
        grid=(images,),
        in_specs=[
            rows_spec(rows, D + LANES),
            rows_spec(rows, D + LANES),
            rows_spec(rows, D),
            rows_spec(rows, D),
            rows_spec(rows, LANES),
            rows_spec(rows, 2),
            rows_spec(rows, D),
            rows_spec(rows, D),
            rows_spec(rows, 3 * width),
            rows_spec(rows, width),
        ]
        + weight_specs(width)
        + [pl.BlockSpec((D, LANES), lambda i: (0, 4 * width // LANES)), whole_spec((1, D))],
        out_specs=[
            rows_spec(rows, D),
            rows_spec(rows, D),
            whole_spec((D, 3 * width)),
            whole_spec((D, width)),
            whole_spec((D, LANES)),
            whole_spec((8, D)),
        ],
        out_shape=[
            jax.ShapeDtypeStruct((tok, D), F32),
            jax.ShapeDtypeStruct((tok, D), BF16),
            jax.ShapeDtypeStruct((D, 3 * width), F32),
            jax.ShapeDtypeStruct((D, width), F32),
            jax.ShapeDtypeStruct((D, LANES), F32),
            jax.ShapeDtypeStruct((8, D), F32),
        ],
        scratch_shapes=[pltpu.VMEM((rows, 3 * width), BF16)],
        compiler_params=params(56),
        name="attn_bwd",
    )(
        own, peer, middle, act_in, gates, ids, grad, normed, packed, heads,
        gathered, gathered, gathered, gain,
    )


def swap_cores(values):
    count = lax.axis_size("tensor")
    return lax.ppermute(values, "tensor", [(i, (i + 1) % count) for i in range(count)])


def add_peer(own, far):
    return (own.astype(F32) + swap_cores(far).astype(F32)).astype(BF16)


def over_shard(values, shards, cap):
    return lax.all_to_all(
        values.reshape(shards, -1, cap, D), "shard", split_axis=0, concat_axis=0, tiled=True
    )


def on_device(
    tokens, routes, w_qkv, w_out, w_router, ln_gain, ln_shift, expert_in, expert_out, cotangent
):
    tok_dev = tokens.shape[0]
    images = tok_dev // SEQ
    rows = round_up(SEQ, 16)
    tok = images * rows
    shards = lax.axis_size("shard")
    exp_dev = expert_in.shape[1]
    experts = exp_dev * shards
    cap = round_up(5 * tok_dev // (2 * experts) + 1, 32)
    half_cap = cap // 2
    slots = experts * half_cap
    core = lax.axis_index("tensor")
    width = w_qkv.shape[3]
    block = w_qkv.shape[1]
    all_rows = ("shard", "dp")

    def padded(values, fill=0):
        values = values.reshape((images, SEQ) + values.shape[1:])
        spare = [(0, 0), (0, rows - SEQ)] + [(0, 0)] * (values.ndim - 2)
        return jnp.pad(values, spare, constant_values=fill).reshape((tok,) + values.shape[2:])

    def trimmed(values):
        return values.reshape(images, rows, D)[:, :SEQ].reshape(tok_dev, D)

    gathered, experts_in, experts_out = [], [], []
    for depth in range(LAYERS):
        small = jnp.concatenate([w_router[depth], ln_gain[depth], ln_shift[depth]], axis=1)
        small = jnp.pad(small, ((0, 0), (0, LANES - small.shape[1])))
        pack = jnp.concatenate(
            [w_qkv[depth].reshape(block, 3 * width), w_out[depth], small], axis=1
        )
        gathered.append(lax.all_gather(pack, all_rows, axis=0, tiled=True))
        experts_in.append(lax.all_gather(expert_in[depth], "dp", axis=1, tiled=True))
        experts_out.append(lax.all_gather(expert_out[depth], "dp", axis=1, tiled=True))

    ids, dest_cols, dest_rows = [], [], []
    before = jnp.tril(jnp.ones((tok, tok), BF16), -1)
    for depth in range(LAYERS):
        id_pad = padded(routes[depth], -1)
        hits = id_pad[:, :, None] == jnp.arange(experts, dtype=jnp.int32)[None, None, :]
        count = jnp.sum(hits.astype(F32), axis=1).astype(BF16)
        earlier = jnp.dot(before, count, preferred_element_type=F32)
        slot = jnp.sum(jnp.where(hits, earlier[:, None, :], 0.0), axis=-1).astype(jnp.int32)
        mine = (id_pad >= 0) & (slot % 2 == core)
        dest = jnp.where(mine, id_pad * half_cap + slot // 2, -1)
        ids.append(id_pad)
        dest_cols.append(dest)
        dest_rows.append(dest.T)

    stream = padded(tokens).astype(F32)
    kept = []
    for depth in range(LAYERS):
        pack = gathered[depth]
        vectors = pack[:, 4 * width + experts : 4 * width + experts + 4].astype(F32).T
        gains = (vectors[0:1], vectors[1:2])
        shifts = (vectors[2:3], vectors[3:4])
        normed, packed, heads, part = attn_fwd(stream, pack, gains[0], shifts[0], images, width)
        middle, act_in, gates, outgoing = mid_fwd(
            stream, part, swap_cores(part), gains[1], shifts[1], pack,
            ids[depth], dest_rows[depth], slots, width,
        )
        received = over_shard(outgoing, shards, half_cap)
        received = (received, swap_cores(received))
        own_y, own_act, own_slope = ffn_fwd(received[0], experts_in[depth], experts_out[depth])
        far_y, far_act, far_slope = ffn_fwd(received[1], experts_in[depth], experts_out[depth])
        act, slope = (own_act, far_act), (own_slope, far_slope)
        returned = over_shard(add_peer(own_y, far_y), shards, half_cap).reshape(slots, D)
        taken, mix = combine_fwd(returned, dest_cols[depth], gates, images)
        kept.append(
            (stream, (middle, act_in, gates, normed, packed, heads), received, act, slope, taken, gains)
        )
        stream = middle + (mix.astype(F32) + swap_cores(mix).astype(F32))
    mixed = trimmed(stream.astype(BF16))

    grad = padded(cotangent).astype(F32)
    big, tiny, in_grads, out_grads = [None] * LAYERS, [None] * LAYERS, [None] * LAYERS, [None] * LAYERS
    for depth in reversed(range(LAYERS)):
        stream_in, saved, received, act, slope, taken, gains = kept[depth]
        grad_out, pgate = spread_bwd(grad, saved[2], taken, dest_rows[depth], slots)
        grad_in = over_shard(grad_out, shards, half_cap)
        if depth + 1 < LAYERS:
            grad_in, in_grads[depth + 1], out_grads[depth + 1] = lax.optimization_barrier(
                (grad_in, in_grads[depth + 1], out_grads[depth + 1])
            )
        grad_in = (grad_in, swap_cores(grad_in))
        own_rows, far_rows, in_grad, down_grad = ffn_bwd(
            received, grad_in, act, slope, experts_in[depth], experts_out[depth]
        )
        in_grads[depth] = lax.psum_scatter(in_grad, "dp", scatter_dimension=1, tiled=True)
        out_grads[depth] = lax.psum_scatter(down_grad, "dp", scatter_dimension=1, tiled=True)
        rows_back = over_shard(add_peer(own_rows, far_rows), shards, half_cap).reshape(slots, D)
        part = gather_bwd(rows_back, dest_cols[depth], pgate, images)
        if depth + 1 < LAYERS:
            part, big[depth + 1], in_grads[depth] = lax.optimization_barrier(
                (part, big[depth + 1], in_grads[depth])
            )
        middle_grad, pnorm, qkv_grad, proj_grad, router_grad, second = attn_bwd(
            part, swap_cores(part), saved, grad, gathered[depth], gains[1], ids[depth], images, width
        )
        normed_grad = pnorm.astype(F32) + swap_cores(pnorm).astype(F32)
        unit, rstd = norm_parts(stream_in)
        grad = middle_grad + norm_back(unit, rstd, gains[0], normed_grad)
        vectors = jnp.stack(
            [jnp.sum(normed_grad * unit, axis=0), second[0], jnp.sum(normed_grad, axis=0), second[1]],
            axis=1,
        )
        tiny[depth] = jnp.concatenate([router_grad[:, :experts], vectors], axis=1)
        big[depth] = lax.psum_scatter(
            jnp.concatenate([qkv_grad.astype(BF16), proj_grad.astype(BF16)], axis=1),
            all_rows, scatter_dimension=0, tiled=True,
        ).astype(F32)
    tiny_all = lax.psum_scatter(
        jnp.concatenate(tiny, axis=1), all_rows, scatter_dimension=0, tiled=True
    ).reshape(block, LAYERS, experts + 4)
    tiny_all = jnp.swapaxes(tiny_all, 0, 1)
    big_all = jnp.stack(big, axis=0)
    return (
        mixed,
        trimmed(grad),
        big_all[:, :, : 3 * width].reshape(LAYERS, block, 3, width),
        big_all[:, :, 3 * width :],
        tiny_all[:, :, :experts],
        tiny_all[:, :, experts : experts + 2],
        tiny_all[:, :, experts + 2],
        tiny_all[:, :, experts + 3],
        jnp.stack(in_grads, axis=0).astype(F32),
        jnp.stack(out_grads, axis=0).astype(F32),
    )


def solution(mesh):
    row_split = P(("shard", "dp"), None)
    mid_split = P(None, ("shard", "dp"), None)
    expert_split = P(None, "shard", "dp", "tensor")
    placed = (
        row_split,
        mid_split,
        P(None, ("shard", "dp"), None, "tensor"),
        P(None, ("shard", "dp"), "tensor"),
        mid_split,
        mid_split,
        mid_split,
        expert_split,
        expert_split,
        row_split,
    )
    return jax.shard_map(
        on_device,
        mesh=mesh,
        in_specs=placed,
        out_specs=(
            row_split,
            row_split,
            P(None, ("shard", "dp"), None, "tensor"),
            P(None, ("shard", "dp"), "tensor"),
            mid_split,
            mid_split,
            P(None, ("shard", "dp")),
            P(None, ("shard", "dp")),
            expert_split,
            expert_split,
        ),
        check_vma=False,
    )
```

time: 2850 us -> 1370 us (0.48)
  waiting for transfers between devices: 1770 us -> 952 us
  blocking collectives: 422 us -> 117 us
  local copies, waits for them, and re-layouts: 274 us -> 48.2 us
  matrix products: 205 us -> 0.84 us
  Pallas kernels: 0 us -> 170 us
  other arithmetic: 125 us -> 44.2 us
    unnamed x33 -> x14, waiting for transfers between devices: 688 us -> 122 us
    reduce_scatter x8 -> x6, waiting for transfers between devices: 873 us -> 437 us  [the longest x2 229 us: on_device(): lax.psum_scatter(jnp.concatenate([qkv_grad.astype(BF16), proj_grad.astype...]
    all_gather x8 -> x0, blocking collectives: 355 us -> none  [the longest x2 96.7 us: on_device(): lax.all_gather(w_router[depth], ('shard', 'dp'), axis=0, tiled=True)]
    dot_general x40 -> x2, matrix products: 198 us -> 0.84 us  [on_device(): earlier = jnp.dot(before, count, preferred_element_type=F32)]
    pallas_call x0 -> x18, Pallas kernels: none -> 170 us  [the longest x2 46.2 us: attn_bwd(): pl.pallas_call(attn_bwd_kernel, grid=(images,), in_specs=[rows_spec(rows,...]
    reshape x28 -> x8, local copies, waits for them, and re-layouts: 105 us -> 4.05 us  [the longest x2 2.56 us: trimmed(): return values.reshape(images, rows, D)[:, :SEQ].reshape(tok_dev, D)]
    all_gather x2, waiting for transfers between devices: 80.8 us -> 179 us  [on_device(): lax.all_gather(expert_out[depth], 'dp', axis=1, tiled=True)]
    all_gather x2, waiting for transfers between devices: 15.2 us -> 101 us  [on_device(): lax.all_gather(expert_in[depth], 'dp', axis=1, tiled=True)]
  transfers between devices with their start and end apart: 33 -> 31, of which waited for: 24 -> 23; matrix products, arithmetic and copies ran while one was open for 12% -> 4% of each run, Pallas kernels for 0% -> 10%
where the time goes in v1:
time: 1370 us; the launch traced here: 1360 us
  waiting for transfers between devices  952 us (69%)
  Pallas kernels  170 us (12%)
  blocking collectives  117 us (9%)
  local copies, waits for them, and re-layouts  48.2 us (4%)
  other arithmetic  44.2 us (3%)
  between operations  15.1 us (1%)
    reduce_scatter x2, waiting for transfers between devices, on_device(): lax.psum_scatter(jnp.concatenate([qkv_grad.astype(BF16), proj_grad.astype...  229 us
    all_gather x2, waiting for transfers between devices, on_device(): lax.all_gather(expert_out[depth], 'dp', axis=1, tiled=True)  179 us
    reduce_scatter x2, waiting for transfers between devices, on_device(): lax.psum_scatter(down_grad, 'dp', scatter_dimension=1, tiled=True)  123 us
    unnamed x14, waiting for transfers between devices  122 us
    all_to_all x6, blocking collectives, over_shard(): lax.all_to_all(values.reshape(shards, -1, cap, D), 'shard', split_axis=0,...  117 us
    all_gather x2, waiting for transfers between devices, on_device(): lax.all_gather(expert_in[depth], 'dp', axis=1, tiled=True)  101 us
    reduce_scatter x2, waiting for transfers between devices, on_device(): lax.psum_scatter(in_grad, 'dp', scatter_dimension=1, tiled=True)  84.7 us
    all_gather x2, waiting for transfers between devices, on_device(): gathered.append(lax.all_gather(pack, all_rows, axis=0, tiled=True))  77.3 us
  transfers between devices with their start and end apart: 31, of which 23 were waited for; matrix products, arithmetic and copies ran while one was open for 4% of the time, Pallas kernels for 10%

profile of v1, /device:TPU:0, one launch (start us, length us, event | category | flops | bytes accessed | tf_op | source)
XLA Modules:
  0.0 1357.6 jit_solution(6413369386824887241)
XLA Ops:
  12.0 3.3 fusion.42
  15.4 1.6 fusion.41
  19.1 59.1 %all-gather.11.cloned.1.call-done.w_ref.wo_ref.small_ref = bf16[768,1664]{1,0:T(8,128)(2,1)} async-done(((bf16[48,1664]{1,0:T(8,128)(2,1)}), bf16[768,1664]{1,0:T(8,128)(2,1)}) %all-gather.11.cloned.1.call-update) | async-done | bytes 2555920 | tf_op jit(solution)/shard_map/all_gather | solution.py:540
  79.5 8.2 attn_fwd.2
  93.3 5.1 mid_fwd.2
  98.4 18.6 %all_to_all.40.x_ref.xa_ref = bf16[4,2,96,768]{3,2,1,0:T(8,128)(2,1)S(1)} all-to-all(bf16[4,2,96,768]{3,2,1,0:T(8,128)(2,1)S(1)} %bitcast.98), channel_id=1, replica_groups=mesh['shard'=4,'dp'=4,'tensor'=2] {'shard'}, dimensions={0} | all-to-all | bytes 2359296 | tf_op jit(solution)/shard_map/all_to_all | solution.py:502
  116.9 51.8 %all-gather.15.cloned.1.call-done = bf16[1,2,768,1536]{3,2,1,0:T(8,128)(2,1)} async-done(((bf16[1,2,192,1536]{3,2,1,0:T(8,128)(2,1)}), bf16[1,2,768,1536]{3,2,1,0:T(8,128)(2,1)}) %all-gather.15.cloned.1.call-update) | async-done | bytes 4718608 | tf_op jit(solution)/shard_map/all_gather | solution.py:541
  168.7 89.5 %all-gather.17.cloned.1.call-done = bf16[1,2,768,1536]{3,2,1,0:T(8,128)(2,1)} async-done(((bf16[1,2,192,1536]{3,2,1,0:T(8,128)(2,1)}), bf16[1,2,768,1536]{3,2,1,0:T(8,128)(2,1)}) %all-gather.17.cloned.1.call-update) | async-done | bytes 4718608 | tf_op jit(solution)/shard_map/all_gather | solution.py:542
  258.2 10.4 ffn_fwd.5
  268.6 1.4 copy-done.23
  270.0 10.0 ffn_fwd.4
  280.3 24.4 %all_to_all.41 = bf16[4,2,96,768]{3,2,1,0:T(8,128)(2,1)S(1)} all-to-all(bf16[4,2,96,768]{3,2,1,0:T(8,128)(2,1)S(1)} %add_convert_fusion.3), channel_id=1, replica_groups=mesh['shard'=4,'dp'=4,'tensor'=2] {'shard'}, dimensions={0} | all-to-all | bytes 2359296 | tf_op jit(solution)/shard_map/all_to_all | solution.py:502
  304.7 2.4 combine_fwd.2
  308.4 18.2 %all-gather.13.cloned.1.call-done.w_ref.wo_ref.small_ref = bf16[768,1664]{1,0:T(8,128)(2,1)} async-done(((bf16[48,1664]{1,0:T(8,128)(2,1)}), bf16[768,1664]{1,0:T(8,128)(2,1)}) %all-gather.13.cloned.1.call-update) | async-done | bytes 2555920 | tf_op jit(solution)/shard_map/all_gather | solution.py:540
  327.9 2.2 fusion.40
  330.1 8.1 attn_fwd.3
  343.7 5.1 mid_fwd.3
  349.5 18.5 %all_to_all.42.x_ref.xa_ref = bf16[4,2,96,768]{3,2,1,0:T(8,128)(2,1)S(1)} all-to-all(bf16[4,2,96,768]{3,2,1,0:T(8,128)(2,1)S(1)} %bitcast.99), channel_id=1, replica_groups=mesh['shard'=4,'dp'=4,'tensor'=2] {'shard'}, dimensions={0} | all-to-all | bytes 2359296 | tf_op jit(solution)/shard_map/all_to_all | solution.py:502
  368.0 49.0 %all-gather.19.cloned.1.call-done = bf16[1,2,768,1536]{3,2,1,0:T(8,128)(2,1)} async-done(((bf16[1,2,192,1536]{3,2,1,0:T(8,128)(2,1)}), bf16[1,2,768,1536]{3,2,1,0:T(8,128)(2,1)}) %all-gather.19.cloned.1.call-update) | async-done | bytes 4718608 | tf_op jit(solution)/shard_map/all_gather | solution.py:541
  417.0 89.9 %all-gather.21.cloned.1.call-done = bf16[1,2,768,1536]{3,2,1,0:T(8,128)(2,1)} async-done(((bf16[1,2,192,1536]{3,2,1,0:T(8,128)(2,1)}), bf16[1,2,768,1536]{3,2,1,0:T(8,128)(2,1)}) %all-gather.21.cloned.1.call-update) | async-done | bytes 4718608 | tf_op jit(solution)/shard_map/all_gather | solution.py:542
  506.9 10.3 ffn_fwd.7
  517.2 1.4 copy-done.25
  518.6 10.0 ffn_fwd.6
  528.6 1.4 copy-done.26
  531.3 4.4 all-to-all-start.3
  536.7 15.0 %all-to-all-done.3 = bf16[4,2,96,768]{3,2,1,0:T(8,128)(2,1)} async-done(((bf16[4,2,96,768]{3,2,1,0:T(8,128)(2,1)}), bf16[4,2,96,768]{3,2,1,0:T(8,128)(2,1)}, u32[]{:S(2)}, u32[]{:S(2)}) %all-to-all-start.3) | async-done | bytes 1179680 | tf_op jit(solution)/shard_map/all_to_all | solution.py:502
  552.7 3.6 combine_fwd.3
  557.3 2.4 spread_bwd.2
  559.7 18.3 %all_to_all.43.da_ref = bf16[4,2,96,768]{3,2,1,0:T(8,128)(2,1)S(1)} all-to-all(bf16[4,2,96,768]{3,2,1,0:T(8,128)(2,1)S(1)} %bitcast.100), channel_id=1, replica_groups=mesh['shard'=4,'dp'=4,'tensor'=2] {'shard'}, dimensions={0} | all-to-all | bytes 2359296 | tf_op jit(solution)/shard_map/all_to_all | solution.py:502
  578.0 2.8 collective-permute-done.8.db_ref
  581.9 21.3 %ffn_bwd.2 = (bf16[4,2,96,768]{3,2,1,0:T(8,128)(2,1)S(1)}, bf16[4,2,96,768]{3,2,1,0:T(8,128)(2,1)S(1)}, bf16[2,768,1536]{2,1,0:T(8,128)(2,1)}, bf16[2,768,1536]{2,1,0:T(8,128)(2,1)}) custom-call(bf16[4,2,96,768]{3,2,1,0:T(8,128)(2,1)S(1)} %copy-done.7, bf16[4,2,96,768]{3,2,1,0:T(8,128)(2,1)} %collective-permute-done.5.x_ref.xb_ref, ...), custom_call_target="tpu_custom_call" | custom-call | tf_op jit(solution)/shard_map/ffn_bwd/pallas_call | solution.py:283
  605.3 2.9 collective-permute-done.9
  608.5 18.8 %all_to_all.44 = bf16[4,2,96,768]{3,2,1,0:T(8,128)(2,1)S(1)} all-to-all(bf16[4,2,96,768]{3,2,1,0:T(8,128)(2,1)S(1)} %add_convert_fusion.1), channel_id=1, replica_groups=mesh['shard'=4,'dp'=4,'tensor'=2] {'shard'}, dimensions={0} | all-to-all | bytes 2359296 | tf_op jit(solution)/shard_map/all_to_all | solution.py:502
  627.4 1.6 gather_bwd.2.own_ref
  629.0 2.7 collective-permute-done.10.peer_ref
  632.8 23.1 %attn_bwd.2 = (f32[624,768]{1,0:T(8,128)}, bf16[624,768]{1,0:T(8,128)(2,1)}, f32[768,1152]{1,0:T(8,128)}, f32[768,384]{1,0:T(8,128)}, f32[768,128]{1,0:T(8,128)}, /*index=5*/f32[8,768]{1,0:T(8,128)}) custom-call(bf16[624,896]{1,0:T(8,128)(2,1)} %copy-done.17, bf16[624,896]{1,0:T(8,128)(2,1)} %copy-done.60, f32[624,768]{1,0:T(8,128)} %get-tuple-element.80.middle_ref, ...), custom_call_target="tpu_custom_call" | custom-call | tf_op jit(solution)/shard_map/attn_bwd/pallas_call | solution.py:450
  655.9 1.3 convert_element_type.153
  657.2 2.2 convert_element_type.152
  659.4 1.6 pad_maximum_fusion
  667.1 2.3 spread_bwd.3
  669.4 18.6 %all_to_all.45.da_ref = bf16[4,2,96,768]{3,2,1,0:T(8,128)(2,1)S(1)} all-to-all(bf16[4,2,96,768]{3,2,1,0:T(8,128)(2,1)S(1)} %bitcast.101), channel_id=1, replica_groups=mesh['shard'=4,'dp'=4,'tensor'=2] {'shard'}, dimensions={0} | all-to-all | bytes 2359296 | tf_op jit(solution)/shard_map/all_to_all | solution.py:502
  688.0 87.4 %reduce-scatter.12.cloned.1.call-done = bf16[2,192,1536]{2,1,0:T(8,128)(2,1)} async-done(((bf16[2,768,1536]{2,1,0:T(8,128)(2,1)}), bf16[2,192,1536]{2,1,0:T(8,128)(2,1)}) %reduce-scatter.12.cloned.1.call-update) | async-done | bytes 1179664 | tf_op jit(solution)/shard_map/reduce_scatter | solution.py:598
  775.4 2.8 collective-permute-done.12.db_ref
  780.5 21.3 %ffn_bwd.3 = (bf16[4,2,96,768]{3,2,1,0:T(8,128)(2,1)S(1)}, bf16[4,2,96,768]{3,2,1,0:T(8,128)(2,1)S(1)}, bf16[2,768,1536]{2,1,0:T(8,128)(2,1)}, bf16[2,768,1536]{2,1,0:T(8,128)(2,1)}) custom-call(bf16[4,2,96,768]{3,2,1,0:T(8,128)(2,1)S(1)} %all_to_all.40.x_ref.xa_ref, bf16[4,2,96,768]{3,2,1,0:T(8,128)(2,1)S(1)} %copy-done.15, ...), custom_call_target="tpu_custom_call" | custom-call | tf_op jit(solution)/shard_map/ffn_bwd/pallas_call | solution.py:283
  805.3 2.7 collective-permute-done.13
  809.3 3.8 all-to-all-start.7
  813.3 99.5 %reduce-scatter.14.cloned.1.call-done = bf16[48,1536]{1,0:T(8,128)(2,1)} async-done(((bf16[768,1536]{1,0:T(8,128)(2,1)}), bf16[48,1536]{1,0:T(8,128)(2,1)}) %reduce-scatter.14.cloned.1.call-update) | async-done | bytes 147472 | tf_op jit(solution)/shard_map/reduce_scatter | solution.py:616
  913.8 1.6 gather_bwd.3.own_ref
  915.4 84.7 %reduce-scatter.16.cloned.1.call-done = bf16[2,192,1536]{2,1,0:T(8,128)(2,1)} async-done(((bf16[2,768,1536]{2,1,0:T(8,128)(2,1)}), bf16[2,192,1536]{2,1,0:T(8,128)(2,1)}) %reduce-scatter.16.cloned.1.call-update) | async-done | bytes 1179664 | tf_op jit(solution)/shard_map/reduce_scatter | solution.py:597
  1000.1 1.4 convert_reduce_fusion
  1001.5 1.4 collective-permute-done.14.peer_ref
  1003.8 23.1 %attn_bwd.3 = (f32[624,768]{1,0:T(8,128)}, bf16[624,768]{1,0:T(8,128)(2,1)}, f32[768,1152]{1,0:T(8,128)}, f32[768,384]{1,0:T(8,128)}, f32[768,128]{1,0:T(8,128)}, /*index=5*/f32[8,768]{1,0:T(8,128)}) custom-call(bf16[624,896]{1,0:T(8,128)(2,1)} %copy-done.16, bf16[624,896]{1,0:T(8,128)(2,1)} %copy-done.59, f32[624,768]{1,0:T(8,128)} %get-tuple-element.73.middle_ref, ...), custom_call_target="tpu_custom_call" | custom-call | tf_op jit(solution)/shard_map/attn_bwd/pallas_call | solution.py:450
  1030.8 3.6 convert_element_type.158
  1035.3 2.3 multiply_reduce_fusion.1
  1038.7 3.2 pad_maximum_fusion.1
  1043.5 2.2 collective-permute-done.7
  1045.7 1.9 add_convert_fusion.4
  1048.8 4.1 maximum_convert_fusion
  1052.9 35.4 %reduce-scatter.20.cloned.1.call-done = bf16[2,192,1536]{2,1,0:T(8,128)(2,1)} async-done(((bf16[2,768,1536]{2,1,0:T(8,128)(2,1)}), bf16[2,192,1536]{2,1,0:T(8,128)(2,1)}) %reduce-scatter.20.cloned.1.call-update) | async-done | bytes 1179664 | tf_op jit(solution)/shard_map/reduce_scatter | solution.py:598
  1088.3 4.3 maximum_convert_fusion.1
  1092.6 1.9 multiply_add_fusion
  1094.7 1.4 reshape.159
  1096.1 119.9 %reduce-scatter.22.cloned.1.call-done = f32[48,24]{1,0:T(8,128)} async-done(((f32[768,24]{1,0:T(8,128)}), f32[48,24]{1,0:T(8,128)}) %reduce-scatter.22.cloned.1.call-update) | async-done | bytes 4624
  1218.6 129.7 %reduce-scatter.18.cloned.1.call-done = bf16[48,1536]{1,0:T(8,128)(2,1)} async-done(((bf16[768,1536]{1,0:T(8,128)(2,1)}), bf16[48,1536]{1,0:T(8,128)(2,1)}) %reduce-scatter.18.cloned.1.call-update) | async-done | bytes 147472 | tf_op jit(solution)/shard_map/reduce_scatter | solution.py:616
  (269 shorter events, 60.1 us)
Async XLA Ops:
  7.2 71.0 %all-gather.11.cloned.1.call-start = ((), (), s32[]{:S(2)}) async-start(), calls=%async_computation.15 | async-start | bytes 2715648 | tf_op jit(solution)/shard_map/all_gather | solution.py:540
  12.0 3.5 copy-start.53
  12.0 156.8 %all-gather.15.cloned.1.call-start = ((), (), s32[]{:S(2)}) async-start(), calls=%async_computation.23 | async-start | bytes 5898240 | tf_op jit(solution)/shard_map/all_gather | solution.py:541
  15.4 242.8 %all-gather.17.cloned.1.call-start = ((), (), s32[]{:S(2)}) async-start(), calls=%async_computation.24 | async-start | bytes 5898240 | tf_op jit(solution)/shard_map/all_gather | solution.py:542
  17.0 309.6 %all-gather.13.cloned.1.call-start = ((), (), s32[]{:S(2)}) async-start(), calls=%async_computation.16 | async-start | bytes 2715648 | tf_op jit(solution)/shard_map/all_gather | solution.py:540
  18.0 399.0 %all-gather.19.cloned.1.call-start = ((), (), s32[]{:S(2)}) async-start(), calls=%async_computation.25 | async-start | bytes 5898240 | tf_op jit(solution)/shard_map/all_gather | solution.py:541
  18.6 488.3 %all-gather.21.cloned.1.call-start = ((), (), s32[]{:S(2)}) async-start(), calls=%async_computation.26 | async-start | bytes 5898240 | tf_op jit(solution)/shard_map/all_gather | solution.py:542
  18.9 60.5 %copy-start.48 = (bf16[3,197,768]{2,1,0:T(8,128)(2,1)}, bf16[3,197,768]{2,1,0:T(8,128)(2,1)S(1)}, u32[]{:S(2)}) copy-start(bf16[3,197,768]{2,1,0:T(8,128)(2,1)S(1)} %reshape.144) | copy-start | bytes 2723332
  19.0 68.6 %copy-start = (f32[3,208,768]{2,1,0:T(8,128)}, f32[3,208,768]{2,1,0:T(8,128)S(1)}, u32[]{:S(2)}) copy-start(f32[3,208,768]{2,1,0:T(8,128)S(1)} %pad_convert_fusion) | copy-start | bytes 5750788
  79.4 13.8 %copy-start.43 = (f32[1,768]{1,0:T(1,128)}, f32[1,768]{1,0:T(1,128)S(1)}, u32[]{:S(2)}) copy-start(f32[1,768]{1,0:T(1,128)S(1)} %get-tuple-element.220.g_ref) | copy-start | bytes 9220
  79.4 11.1 copy-start.64
  90.5 2.7 collective-permute-start
  90.8 7.5 copy-start.8
  92.0 212.7 %copy-start.10 = (s32[624,2]{1,0:T(8,128)}, s32[624,2]{1,0:T(8,128)S(1)}, u32[]{:S(2)}) copy-start(s32[624,2]{1,0:T(8,128)S(1)} %fusion.20.dest_ref) | copy-start | bytes 14980
  98.4 18.6 %copy-start.36 = (bf16[624,768]{1,0:T(8,128)(2,1)}, bf16[624,768]{1,0:T(8,128)(2,1)S(1)}, u32[]{:S(2)}) copy-start(bf16[624,768]{1,0:T(8,128)(2,1)S(1)} %get-tuple-element.117.act_ref) | copy-start | bytes 2875396
  98.4 206.4 %copy-start.18 = (f32[624,128]{1,0:T(8,128)}, f32[624,128]{1,0:T(8,128)S(1)}, u32[]{:S(2)}) copy-start(f32[624,128]{1,0:T(8,128)S(1)} %get-tuple-element.77.gates_ref) | copy-start | bytes 958468
  116.9 141.3 %collective-permute-start.1 = (bf16[4,2,96,768]{3,2,1,0:T(8,128)(2,1)S(1)}, bf16[4,2,96,768]{3,2,1,0:T(8,128)(2,1)S(1)}, u32[]{:S(2)}, u32[]{:S(2)}) collective-permute-start(bf16[4,2,96,768]{3,2,1,0:T(8,128)(2,1)S(1)} %all_to_all.40.x_ref.xa_ref), channel_id=1, source_target_pairs={{0,1},{1,0},{2,3},{3,2},{4,5},{5,4},{6,7},{7,6},{8,9},{9,8},{10,11... | collective-permute-start | bytes 3538952 | tf_op jit(solution)/shard_map/ppermute | solution.py:494
  258.2 10.4 copy-start.14
  270.0 10.0 collective-permute-start.2
  280.0 24.8 %copy-start.24 = (bf16[4,2,96,1536]{3,2,1,0:T(8,128)(2,1)}, bf16[4,2,96,1536]{3,2,1,0:T(8,128)(2,1)S(1)}, u32[]{:S(2)}) copy-start(bf16[4,2,96,1536]{3,2,1,0:T(8,128)(2,1)S(1)} %get-tuple-element.106.acta_ref) | copy-start | bytes 7077892
  308.4 19.4 %collective-permute-start.3 = (bf16[624,768]{1,0:T(8,128)(2,1)S(1)}, bf16[624,768]{1,0:T(8,128)(2,1)}, u32[]{:S(2)}, u32[]{:S(2)}) collective-permute-start(bf16[624,768]{1,0:T(8,128)(2,1)S(1)} %get-tuple-element.78), channel_id=1, source_target_pairs={{0,1},{1,0},{2,3},{3,2},{4,5},{5,4},{6,7},{7,6},{8,9},{9,8},{10,11... | collective-permute-start | bytes 2875400 | tf_op jit(solution)/shard_map/ppermute | solution.py:494
  327.8 15.9 %copy-start.44 = (f32[1,768]{1,0:T(1,128)}, f32[1,768]{1,0:T(1,128)S(1)}, u32[]{:S(2)}) copy-start(f32[1,768]{1,0:T(1,128)S(1)} %get-tuple-element.225.g_ref) | copy-start | bytes 9220
  330.1 8.1 copy-start.2
  341.0 2.7 collective-permute-start.4
  341.3 7.4 copy-start.9
  342.5 6.2 copy-start.12
  349.5 18.5 %copy-start.38 = (bf16[624,768]{1,0:T(8,128)(2,1)}, bf16[624,768]{1,0:T(8,128)(2,1)S(1)}, u32[]{:S(2)}) copy-start(bf16[624,768]{1,0:T(8,128)(2,1)S(1)} %get-tuple-element.95.act_ref) | copy-start | bytes 2875396
  368.0 150.6 %copy-start.6 = (bf16[4,2,96,768]{3,2,1,0:T(8,128)(2,1)}, bf16[4,2,96,768]{3,2,1,0:T(8,128)(2,1)S(1)}, u32[]{:S(2)}) copy-start(bf16[4,2,96,768]{3,2,1,0:T(8,128)(2,1)S(1)} %all_to_all.42.x_ref.xa_ref) | copy-start | bytes 3538948
  368.0 138.9 %collective-permute-start.5 = (bf16[4,2,96,768]{3,2,1,0:T(8,128)(2,1)S(1)}, bf16[4,2,96,768]{3,2,1,0:T(8,128)(2,1)}, u32[]{:S(2)}, u32[]{:S(2)}) collective-permute-start(bf16[4,2,96,768]{3,2,1,0:T(8,128)(2,1)S(1)} %all_to_all.42.x_ref.xa_ref), channel_id=1, source_target_pairs={{0,1},{1,0},{2,3},{3,2},{4,5},{5,4},{6,7},{7,6},{8,9},{9,8},{10,11... | collective-permute-start | bytes 3538952 | tf_op jit(solution)/shard_map/ppermute | solution.py:494
  518.6 11.4 collective-permute-start.6
  531.3 4.9 copy-start.62
  531.3 20.4 %all-to-all-start.3 = ((bf16[4,2,96,768]{3,2,1,0:T(8,128)(2,1)}), bf16[4,2,96,768]{3,2,1,0:T(8,128)(2,1)}, u32[]{:S(2)}, u32[]{:S(2)}) async-start(bf16[4,2,96,768]{3,2,1,0:T(8,128)(2,1)} %add_convert_fusion.2), calls=%async_computation.3 | async-start | bytes 2359296 | tf_op jit(solution)/shard_map/all_to_all | solution.py:502
  535.7 152.3 %reduce-scatter.10.cloned.1.call-start = ((), (), s32[]{:S(2)}) async-start(), calls=%async_computation.17 | async-start | bytes 5898240 | tf_op jit(solution)/shard_map/reduce_scatter | solution.py:597
  536.4 15.3 %copy-start.13 = (s32[624,2]{1,0:T(8,128)S(1)}, s32[624,2]{1,0:T(8,128)}, u32[]{:S(2)}) copy-start(s32[624,2]{1,0:T(8,128)} %copy-done.12) | copy-start | bytes 14980
  536.7 23.0 %copy-start.5 = (f32[624,768]{1,0:T(8,128)}, f32[624,768]{1,0:T(8,128)S(1)}, u32[]{:S(2)}) copy-start(f32[624,768]{1,0:T(8,128)S(1)} %bitcast_convert_fusion.grad_ref) | copy-start | bytes 5750788
  552.7 4.6 copy-start.22
  559.7 21.1 %copy-start.41 = (bf16[624,128]{1,0:T(8,128)(2,1)}, bf16[624,128]{1,0:T(8,128)(2,1)S(1)}, u32[]{:S(2)}) copy-start(bf16[624,128]{1,0:T(8,128)(2,1)S(1)} %get-tuple-element.94.pgate_ref) | copy-start | bytes 479236
  559.7 22.2 %copy-start.7 = (bf16[4,2,96,768]{3,2,1,0:T(8,128)(2,1)S(1)}, bf16[4,2,96,768]{3,2,1,0:T(8,128)(2,1)}, u32[]{:S(2)}) copy-start(bf16[4,2,96,768]{3,2,1,0:T(8,128)(2,1)} %copy-done.6) | copy-start | bytes 3538948
  578.0 2.8 collective-permute-start.8
  604.3 171.1 %reduce-scatter.12.cloned.1.call-start = ((), (), s32[]{:S(2)}) async-start(), calls=%async_computation.18 | async-start | bytes 5898240 | tf_op jit(solution)/shard_map/reduce_scatter | solution.py:598
  605.0 307.8 %reduce-scatter.14.cloned.1.call-start = ((), (), s32[]{:S(2)}) async-start(), calls=%async_computation.19 | async-start | bytes 2506752 | tf_op jit(solution)/shard_map/reduce_scatter | solution.py:616
  605.1 3.1 collective-permute-start.9
  608.5 18.9 %copy-start.42 = (bf16[624,128]{1,0:T(8,128)(2,1)S(1)}, bf16[624,128]{1,0:T(8,128)(2,1)}, u32[]{:S(2)}) copy-start(bf16[624,128]{1,0:T(8,128)(2,1)} %copy-done.41) | copy-start | bytes 479236
  629.0 2.8 collective-permute-start.10
  661.0 339.0 %reduce-scatter.16.cloned.1.call-start = ((), (), s32[]{:S(2)}) async-start(), calls=%async_computation.20 | async-start | bytes 5898240 | tf_op jit(solution)/shard_map/reduce_scatter | solution.py:597
  661.1 2.8 collective-permute-start.11
  775.4 2.8 collective-permute-start.12
  803.8 284.5 %reduce-scatter.20.cloned.1.call-start = ((), (), s32[]{:S(2)}) async-start(), calls=%async_computation.22 | async-start | bytes 5898240 | tf_op jit(solution)/shard_map/reduce_scatter | solution.py:598
  803.9 4.1 copy-start.32
  805.2 2.8 collective-permute-start.13
  809.3 104.5 %copy-start.11 = (s32[624,2]{1,0:T(8,128)S(1)}, s32[624,2]{1,0:T(8,128)}, u32[]{:S(2)}) copy-start(s32[624,2]{1,0:T(8,128)} %copy-done.10) | copy-start | bytes 14980
  809.3 104.5 %all-to-all-start.7 = ((bf16[4,2,96,768]{3,2,1,0:T(8,128)(2,1)}), bf16[4,2,96,768]{3,2,1,0:T(8,128)(2,1)S(1)}, u32[]{:S(2)}, u32[]{:S(2)}) async-start(bf16[4,2,96,768]{3,2,1,0:T(8,128)(2,1)} %add_convert_fusion), calls=%async_computation.9 | async-start | bytes 2359296 | tf_op jit(solution)/shard_map/all_to_all | solution.py:502
  813.1 402.9 %reduce-scatter.22.cloned.1.call-start = ((), (), s32[]{:S(2)}) async-start(), calls=%async_computation.27 | async-start | bytes 417792
  915.4 87.4 %copy-start.16 = (bf16[624,896]{1,0:T(8,128)(2,1)}, bf16[624,896]{1,0:T(8,128)(2,1)S(1)}, u32[]{:S(2)}) copy-start(bf16[624,896]{1,0:T(8,128)(2,1)S(1)} %gather_bwd.3.own_ref) | copy-start | bytes 3354628
  1000.1 2.8 collective-permute-start.14
  1003.8 23.4 %copy-start.49 = (bf16[3,197,768]{2,1,0:T(8,128)(2,1)S(1)}, bf16[3,197,768]{2,1,0:T(8,128)(2,1)}, u32[]{:S(2)}) copy-start(bf16[3,197,768]{2,1,0:T(8,128)(2,1)} %copy-done.48) | copy-start | bytes 2723332
  1003.8 24.0 %copy-start.63 = (f32[768,128]{1,0:T(8,128)S(1)}, f32[768,128]{1,0:T(8,128)}, u32[]{:S(2)}) copy-start(f32[768,128]{1,0:T(8,128)} %get-tuple-element.128) | copy-start | bytes 1179652
  1027.0 8.3 collective-permute-start.15
  1030.8 4.5 copy-start.1
  1030.8 4.5 copy-start.50
  1038.7 309.6 %reduce-scatter.18.cloned.1.call-start = ((), (), s32[]{:S(2)}) async-start(), calls=%async_computation.21 | async-start | bytes 2506752 | tf_op jit(solution)/shard_map/reduce_scatter | solution.py:616
  1043.2 2.5 collective-permute-start.7
  1088.3 4.3 copy-start.51
  1088.3 4.3 copy-start.54
  (32 other events, 43.7 us)
Sparse Core Ops, SparseCore 0:
  12.1 66.0 all-gather.10
  80.3 88.3 all-gather.14
  170.3 87.8 all-gather.16
  261.4 65.1 all-gather.12
  328.6 88.3 all-gather.18
  419.0 87.8 all-gather.20
  604.4 82.2 reduce-scatter.9
  689.5 85.7 reduce-scatter.11
  780.3 132.5 reduce-scatter.13
  915.7 84.3 reduce-scatter.15
  1002.5 85.7 reduce-scatter.19
  1094.1 121.8 reduce-scatter.21
  1220.9 127.2 reduce-scatter.17
